TPU v7x, 128 devices: a whole 4x4x4 slice. The times are simulated.
128 devices in a mesh: grp: 4 (over x_lo, core), tp: 32 (over y, x_hi, z).
Axes of the slice: x: 4 (x_hi: 2, x_lo: 2; x = x_hi * 2 + x_lo), y: 4, z: 4, core: 2. Of those that a mesh axis runs over, the one named last changes fastest.
Arguments:
- queries: bfloat16 [128, 16, 2048], P(('grp', 'tp')), may hold values from -36 to 36
- cache_keys: bfloat16 [128, 16, 2048, 128], P(('grp', 'tp')), may hold values from -7.5 to 7.5
- cache_values: bfloat16 [128, 16, 2048, 128], P(('grp', 'tp')), may hold values from -24 to 24
- lengths: int32 [256], replicated, may hold values from 512 to 2048
- old_tiles: bfloat16 [128, 128, 128, 128], P(('grp', 'tp')), may hold values from -0.046875 to 0.046875
- old_scales: bfloat16 [128, 128, 128], P(('grp', 'tp')), may hold values from 0.29882812 to 3
- slot_tiles: int32 [128, 128], replicated, may hold values from 0 to 16383, as said below
Outputs:
- projected: bfloat16 [256, 16384], P('tp', 'grp')
Inputs may be any that keep to these rules, and one draw needn't show every extreme that they name: Each row of slot_tiles names exactly one tile of each new owner n (tile numbers n * 128 to n * 128 + 127), and every tile number stands exactly once in the whole table.
All inputs are finite; a program needn't handle non-finite values.
Results may differ from a plain program's by a relative error of at most 0.03.
Values may be sent and summed in bfloat16 or wider, within the bound.
A program may use at most 128 MiB of HBM per device.

v0:
```python
import jax
import jax.numpy as jnp
from jax import lax
from jax.sharding import PartitionSpec as P

D = 16384
KV_HEADS = 8
HEAD_DIM = 128
GROUP_HEADS = 16


def attend_rows(queries_one, keys_one, values_one, live_len):
    row_count = queries_one.shape[0]
    per_head = queries_one.reshape(row_count, GROUP_HEADS, HEAD_DIM)
    scores = jnp.einsum(
        "rhd,rld->rhl", per_head, keys_one, preferred_element_type=jnp.float32
    ) * HEAD_DIM ** (-0.5)
    inside = lax.broadcasted_iota(jnp.int32, scores.shape, 2) < live_len[:, None, None]
    scores = jnp.where(inside, scores, -1e30)
    row_max = jnp.max(scores, axis=2, keepdims=True)
    weights = jnp.where(inside, jnp.exp(scores - row_max), 0.0)
    row_sum = jnp.sum(weights, axis=2, keepdims=True)
    attn_weights = (weights / row_sum).astype(jnp.bfloat16)
    mixed_out = jnp.einsum(
        "rhl,rld->rhd", attn_weights, values_one, preferred_element_type=jnp.float32
    )
    return mixed_out.astype(jnp.bfloat16).reshape(row_count, GROUP_HEADS * HEAD_DIM)


def body(queries, cache_keys, cache_values, lengths, old_tiles, old_scales, slot_tiles):
    groups = lax.axis_size("grp")
    tp_count = lax.axis_size("tp")
    devices = groups * tp_count
    myself = lax.axis_index("grp") * tp_count + lax.axis_index("tp")
    group_rows = queries.shape[1]
    first_row = myself // KV_HEADS * group_rows
    live_len = lax.dynamic_slice_in_dim(lengths, first_row, group_rows)
    attended = attend_rows(queries[0], cache_keys[0], cache_values[0], live_len)
    slice_width = GROUP_HEADS * HEAD_DIM // tp_count
    old_groups = tp_count // KV_HEADS
    arrived = lax.all_to_all(attended, "tp", split_axis=1, concat_axis=0, tiled=True)
    regrouped = arrived.reshape(old_groups, KV_HEADS, group_rows, slice_width)
    regrouped = regrouped.transpose(0, 2, 1, 3).reshape(
        old_groups * group_rows, KV_HEADS * slice_width
    )
    features = lax.all_gather(regrouped, "grp", axis=0, tiled=True)
    tile_rows = old_tiles.shape[2]
    tile_cols = old_tiles.shape[3]
    my_slots = lax.dynamic_index_in_dim(slot_tiles, myself, 0, keepdims=False)
    by_owner = jnp.argsort(my_slots // devices)
    send_tiles = old_tiles[0][by_owner]
    send_scales = old_scales[0][by_owner]
    got_tiles, got_scales = (
        lax.all_to_all(send_tiles, ("grp", "tp"), split_axis=0, concat_axis=0, tiled=True),
        lax.all_to_all(send_scales, ("grp", "tp"), split_axis=0, concat_axis=0, tiled=True),
    )
    matches = slot_tiles // devices == myself
    local_index = jnp.sum(jnp.where(matches, slot_tiles % devices, 0), axis=1)
    arrange = jnp.argsort(local_index)
    placed = got_tiles[arrange]
    scales = got_scales[arrange]
    dequant = (placed.astype(jnp.float32) * scales.astype(jnp.float32)[:, :, None]).astype(
        jnp.bfloat16
    )
    block_cols = D // groups
    col_tiles = block_cols // tile_cols
    row_tiles = devices // col_tiles
    new_block = dequant.reshape(row_tiles, col_tiles, tile_rows, tile_cols).transpose(0, 2, 1, 3)
    new_block = new_block.reshape(row_tiles * tile_rows, col_tiles * tile_cols)
    product = jnp.dot(features, new_block, preferred_element_type=jnp.float32)
    return lax.psum_scatter(
        product.astype(jnp.bfloat16).astype(jnp.float32).astype(jnp.bfloat16),
        "tp",
        scatter_dimension=0,
        tiled=True,
    )


def solution(mesh):
    return jax.shard_map(
        body,
        mesh=mesh,
        in_specs=(
            P(("grp", "tp"), None, None),
            P(("grp", "tp"), None, None, None),
            P(("grp", "tp"), None, None, None),
            P(),
            P(("grp", "tp"), None, None, None),
            P(("grp", "tp"), None, None),
            P(),
        ),
        out_specs=P("tp", "grp"),
        check_vma=False,
    )
```

profile of v0, /device:TPU:0, one launch (start us, length us, event | category | flops | bytes accessed | tf_op | source)
XLA Modules:
  0.0 326.6 jit_solution(11436274888082886892)
XLA Ops:
  6.5 0.7 and_select_fusion
  7.2 2.5 sort.31
  9.8 0.7 gather_fusion.2
  10.5 0.7 copy.21
  11.2 11.1 %all-to-all-start.2 = ((bf16[128,1,128]{2,1,0:T(2,128)(2,1)}), bf16[128,1,128]{2,1,0:T(2,128)(2,1)S(1)}, u32[]{:S(2)}, u32[]{:S(2)}) async-start(bf16[128,1,128]{2,1,0:T(2,128)(2,1)} %copy.21), calls=%async_computation.2 | async-start | bytes 131072 | tf_op jit(solution)/shard_map/all_to_all | solution.py:55
  22.4 0.9 copy.25
  23.2 0.8 dynamic_slice.7
  24.0 5.0 %fusion.26 = (f32[16,16]{1,0:T(8,128)S(1)}, f32[16,16,2048]{2,1,0:T(8,128)S(1)}) fusion(s32[16]{0:T(128)S(1)} %dynamic_slice.7, bf16[16,16,128]{2,1,0:T(8,128)(2,1)S(1)} %bitcast.61, bf16[1,16,2048,128]{3,2,1,0:T(8,128)(2,1)} %param.8), kind=kOutput, calls=%fused_computation.44 | convolution fusion | flops 137889792 | bytes 10552384 | tf_op jit(solution)/shard_map/sub | solution.py:21
  29.0 4.7 %fusion.17 = bf16[16,16,128]{2,1,0:T(8,128)(2,1)S(1)} fusion(bf16[1,16,2048,128]{3,2,1,0:T(8,128)(2,1)} %param.9, f32[16,16,2048]{2,1,0:T(8,128)S(1)} %get-tuple-element.10, f32[16,16]{1,0:T(8,128)S(1)} %get-tuple-element.9), kind=kOutput, calls=%fused_computation.21 | convolution fusion | flops 135299072 | bytes 10552320 | tf_op jit(solution)/shard_map/rhl,rld->rhd/dot_general | solution.py:24
  33.6 0.1 all_to_all.23
  33.8 0.1 copy.37
  33.8 0.8 reshape.73
  34.6 0.0 all-to-all-done.2
  34.6 9.5 %all-to-all-start = ((bf16[32,2,512]{2,1,0:T(2,128)(2,1)}), bf16[32,2,512]{2,1,0:T(2,128)(2,1)S(1)}, u32[]{:S(2)}, u32[]{:S(2)}) async-start(bf16[32,2,512]{2,1,0:T(2,128)(2,1)} %reshape.73), calls=%async_computation | async-start | bytes 131072 | tf_op jit(solution)/shard_map/all_to_all | solution.py:41
  44.1 5.2 %gather_fusion = bf16[128,128,128]{2,1,0:T(8,128)(2,1)} fusion(bf16[128,128,128]{2,1,0:T(8,128)(2,1)} %bitcast.57, s32[1024]{0:T(1024)S(1)} %pad_clamp_fusion.1), kind=kCustom, calls=%fused_computation | custom fusion | bytes 8389120 | tf_op jit(solution)/shard_map/gather | solution.py:51
  49.3 4.7 %all-to-all-done = bf16[32,2,512]{2,1,0:T(2,128)(2,1)S(1)} async-done(((bf16[32,2,512]{2,1,0:T(2,128)(2,1)}), bf16[32,2,512]{2,1,0:T(2,128)(2,1)S(1)}, u32[]{:S(2)}, u32[]{:S(2)}) %all-to-all-start) | async-done | bytes 65568 | tf_op jit(solution)/shard_map/all_to_all | solution.py:41
  54.1 5.9 %all-to-all-start.1 = ((bf16[128,128,128]{2,1,0:T(8,128)(2,1)}), bf16[128,128,128]{2,1,0:T(8,128)(2,1)}, u32[]{:S(2)}, u32[]{:S(2)}) async-start(bf16[128,128,128]{2,1,0:T(8,128)(2,1)} %gather_fusion), calls=%async_computation.1 | async-start | bytes 8388608 | tf_op jit(solution)/shard_map/all_to_all | solution.py:54
  59.9 0.0 reduce-scatter.2.cloned.1.call-start
  60.0 0.1 fusion.23
  60.2 2.5 sort.32
  62.7 0.7 gather_fusion.3
  63.4 0.1 copy.22
  63.5 0.1 reshape.74
  63.7 0.1 reshape.33
  63.9 44.0 %all_gather.3 = bf16[256,512]{1,0:T(8,128)(2,1)S(1)} all-gather(bf16[64,512]{1,0:T(8,128)(2,1)S(1)} %reshape.33), channel_id=1, replica_groups=mesh['grp'=4,'tp'=32] {'grp'}, dimensions={0}, use_global_device_ids=true | all-gather | bytes 327680 | tf_op jit(solution)/shard_map/all_gather | solution.py:46
  107.9 4.5 %all-to-all-done.1 = bf16[128,128,128]{2,1,0:T(8,128)(2,1)} async-done(((bf16[128,128,128]{2,1,0:T(8,128)(2,1)}), bf16[128,128,128]{2,1,0:T(8,128)(2,1)}, u32[]{:S(2)}, u32[]{:S(2)}) %all-to-all-start.1) | async-done | bytes 4194336 | tf_op jit(solution)/shard_map/all_to_all | solution.py:54
  112.5 5.2 %gather_fusion.1 = bf16[128,128,128]{2,1,0:T(8,128)(2,1)} fusion(bf16[128,128,128]{2,1,0:T(8,128)(2,1)} %all-to-all-done.1, s32[1024]{0:T(1024)S(1)} %pad_clamp_fusion), kind=kCustom, calls=%fused_computation.1 | custom fusion | bytes 8389120 | tf_op jit(solution)/shard_map/gather | solution.py:60
  117.7 3.3 convert.2
  121.0 11.2 %fusion.5 = bf16[4,32,128,128]{3,1,2,0:T(8,128)(2,1)S(1)} fusion(f32[4,32,128,128]{3,2,1,0:T(8,128)S(1)} %convert.2, f32[4,32,128]{1,2,0:T(8,128)S(1)} %copy.22), kind=kLoop, calls=%fused_computation.10 | loop fusion | flops 4194304 | bytes 12648448 | tf_op jit(solution)/shard_map/convert_element_type | solution.py:62
  132.1 3.0 convolution_convert_fusion
  135.2 0.0 reduce-scatter.2.cloned.1.call-update
  135.2 184.5 %reduce-scatter.2.cloned.1.call-done = bf16[8,4096]{1,0:T(8,128)(2,1)} async-done(((bf16[256,4096]{1,0:T(8,128)(2,1)}), bf16[8,4096]{1,0:T(8,128)(2,1)}) %reduce-scatter.2.cloned.1.call-update) | async-done | bytes 65552 | tf_op jit(solution)/shard_map/reduce_scatter | solution.py:71
  (12 shorter events, 0.1 us)
Async XLA Ops:
  6.5 3.3 copy-start
  11.2 23.4 %all-to-all-start.2 = ((bf16[128,1,128]{2,1,0:T(2,128)(2,1)}), bf16[128,1,128]{2,1,0:T(2,128)(2,1)S(1)}, u32[]{:S(2)}, u32[]{:S(2)}) async-start(bf16[128,1,128]{2,1,0:T(2,128)(2,1)} %copy.21), calls=%async_computation.2 | async-start | bytes 131072 | tf_op jit(solution)/shard_map/all_to_all | solution.py:55
  34.6 19.5 %all-to-all-start = ((bf16[32,2,512]{2,1,0:T(2,128)(2,1)}), bf16[32,2,512]{2,1,0:T(2,128)(2,1)S(1)}, u32[]{:S(2)}, u32[]{:S(2)}) async-start(bf16[32,2,512]{2,1,0:T(2,128)(2,1)} %reshape.73), calls=%async_computation | async-start | bytes 131072 | tf_op jit(solution)/shard_map/all_to_all | solution.py:41
  49.3 10.7 %copy-start.1 = (s32[128,128]{1,0:T(8,128)S(1)}, s32[128,128]{1,0:T(8,128)}, u32[]{:S(2)}) copy-start(s32[128,128]{1,0:T(8,128)} %param.13) | copy-start | bytes 196612
  54.1 58.4 %all-to-all-start.1 = ((bf16[128,128,128]{2,1,0:T(8,128)(2,1)}), bf16[128,128,128]{2,1,0:T(8,128)(2,1)}, u32[]{:S(2)}, u32[]{:S(2)}) async-start(bf16[128,128,128]{2,1,0:T(8,128)(2,1)} %gather_fusion), calls=%async_computation.1 | async-start | bytes 8388608 | tf_op jit(solution)/shard_map/all_to_all | solution.py:54
  59.9 259.8 %reduce-scatter.2.cloned.1.call-start = ((), (), s32[]{:S(2)}) async-start(), calls=%async_computation.4 | async-start | bytes 2162688 | tf_op jit(solution)/shard_map/reduce_scatter | solution.py:71
Sparse Core Ops, SparseCore 0:
  135.3 184.3 reduce-scatter.1
where the time goes:
time: 327 us
  waiting for transfers between devices  194 us (59%)
  blocking collectives  44 us (13%)
  starting transfers between devices  26.5 us (8%)
  other arithmetic  20.4 us (6%)
  local copies, waits for them, and re-layouts  15.6 us (5%)
  between operations  13.5 us (4%)
  matrix products  12.7 us (4%)
    reduce_scatter x1, waiting for transfers between devices, body(): lax.psum_scatter(product.astype(jnp.bfloat16).astype(jnp.float32).astype(...  185 us
    all_gather x1, blocking collectives, body(): features = lax.all_gather(regrouped, 'grp', axis=0, tiled=True)  44 us
    convert_element_type x1, other arithmetic, body(): (placed.astype(jnp.float32) * scales.astype(jnp.float32)[:, :, None]).ast...  11.2 us
    all_to_all x1, starting transfers between devices, body(): lax.all_to_all(send_scales, ('grp', 'tp'), split_axis=0, concat_axis=0, t...  11.1 us
    all_to_all x1, starting transfers between devices, body(): lax.all_to_all(attended, 'tp', split_axis=1, concat_axis=0, tiled=True)  9.5 us
  transfers between devices with their start and end apart: 4, of which 3 were waited for; matrix products, arithmetic and copies ran while one was open for 6% of the time, Pallas kernels for 0%

commit v1 on v0

--- a/solution.py
+++ b/solution.py
@@ -37,13 +37,14 @@
     live_len = lax.dynamic_slice_in_dim(lengths, first_row, group_rows)
     attended = attend_rows(queries[0], cache_keys[0], cache_values[0], live_len)
     slice_width = GROUP_HEADS * HEAD_DIM // tp_count
-    old_groups = tp_count // KV_HEADS
-    arrived = lax.all_to_all(attended, "tp", split_axis=1, concat_axis=0, tiled=True)
-    regrouped = arrived.reshape(old_groups, KV_HEADS, group_rows, slice_width)
-    regrouped = regrouped.transpose(0, 2, 1, 3).reshape(
-        old_groups * group_rows, KV_HEADS * slice_width
+    pieces = attended.reshape(group_rows, tp_count, slice_width).transpose(1, 0, 2)
+    pieces = jnp.broadcast_to(pieces[None], (groups, tp_count, group_rows, slice_width))
+    pieces = pieces.reshape(devices, group_rows, slice_width)
+    arrived = lax.all_to_all(pieces, ("grp", "tp"), split_axis=0, concat_axis=0, tiled=True)
+    features = arrived.reshape(devices // KV_HEADS, KV_HEADS, group_rows, slice_width)
+    features = features.transpose(0, 2, 1, 3).reshape(
+        devices // KV_HEADS * group_rows, KV_HEADS * slice_width
     )
-    features = lax.all_gather(regrouped, "grp", axis=0, tiled=True)
     tile_rows = old_tiles.shape[2]
     tile_cols = old_tiles.shape[3]
     my_slots = lax.dynamic_index_in_dim(slot_tiles, myself, 0, keepdims=False)
@@ -68,12 +69,9 @@
     new_block = dequant.reshape(row_tiles, col_tiles, tile_rows, tile_cols).transpose(0, 2, 1, 3)
     new_block = new_block.reshape(row_tiles * tile_rows, col_tiles * tile_cols)
     product = jnp.dot(features, new_block, preferred_element_type=jnp.float32)
-    return lax.psum_scatter(
-        product.astype(jnp.bfloat16).astype(jnp.float32).astype(jnp.bfloat16),
-        "tp",
-        scatter_dimension=0,
-        tiled=True,
-    )
+    terms = product.astype(jnp.bfloat16).reshape(tp_count, -1, block_cols)
+    terms = lax.all_to_all(terms, "tp", split_axis=0, concat_axis=0, tiled=True)
+    return jnp.sum(terms.astype(jnp.float32), axis=0).astype(jnp.bfloat16)
 
 
 def solution(mesh):

time: 327 us -> 163 us (0.50)
  waiting for transfers between devices: 194 us -> 53.8 us
  between operations: 13.5 us -> 0.16 us
  blocking collectives: 44 us -> 32.8 us
    reduce_scatter x1 -> x0, waiting for transfers between devices: 185 us -> none  [body(): lax.psum_scatter(product.astype(jnp.bfloat16).astype(jnp.float32).astype(...]
    all_gather x1 -> x0, blocking collectives: 44 us -> none  [body(): features = lax.all_gather(regrouped, 'grp', axis=0, tiled=True)]
    all_to_all x1, waiting for transfers between devices: 4.55 us -> 48.1 us  [body(): lax.all_to_all(send_tiles, ('grp', 'tp'), split_axis=0, concat_axis=0, ti...]
    all_to_all x0 -> x1, blocking collectives: none -> 32.8 us  [body(): terms = lax.all_to_all(terms, 'tp', split_axis=0, concat_axis=0, tiled=True)]
  transfers between devices with their start and end apart: 4 -> 3, of which waited for: 3 -> 2; matrix products, arithmetic and copies ran while one was open for 6% -> 14% of each run, Pallas kernels for 0% -> 0%
where the time goes in v1:
time: 163 us; the launch traced here: 162 us
  waiting for transfers between devices  53.8 us (33%)
  blocking collectives  32.8 us (20%)
  starting transfers between devices  26.7 us (16%)
  other arithmetic  21.3 us (13%)
  local copies, waits for them, and re-layouts  16.3 us (10%)
  matrix products  11.3 us (7%)
    all_to_all x1, waiting for transfers between devices, body(): lax.all_to_all(send_tiles, ('grp', 'tp'), split_axis=0, concat_axis=0, ti...  48.1 us
    all_to_all x1, blocking collectives, body(): terms = lax.all_to_all(terms, 'tp', split_axis=0, concat_axis=0, tiled=True)  32.8 us
    convert_element_type x1, other arithmetic, body(): (placed.astype(jnp.float32) * scales.astype(jnp.float32)[:, :, None]).ast...  11.2 us
    all_to_all x1, starting transfers between devices, body(): lax.all_to_all(send_scales, ('grp', 'tp'), split_axis=0, concat_axis=0, t...  11.1 us
    all_to_all x1, starting transfers between devices, body(): lax.all_to_all(pieces, ('grp', 'tp'), split_axis=0, concat_axis=0, tiled=...  9.76 us
    all_to_all x1, starting transfers between devices, body(): lax.all_to_all(send_tiles, ('grp', 'tp'), split_axis=0, concat_axis=0, ti...  5.82 us
    all_to_all x1, waiting for transfers between devices, body(): lax.all_to_all(pieces, ('grp', 'tp'), split_axis=0, concat_axis=0, tiled=...  5.66 us
    gather x1, local copies, waits for them, and re-layouts, body(): send_tiles = old_tiles[0][by_owner]  5.24 us
  transfers between devices with their start and end apart: 3, of which 2 were waited for; matrix products, arithmetic and copies ran while one was open for 14% of the time, Pallas kernels for 0%

profile of v1, /device:TPU:0, one launch (start us, length us, event | category | flops | bytes accessed | tf_op | source)
XLA Modules:
  0.0 162.4 jit_solution(7049767147739375034)
XLA Ops:
  0.0 0.7 and_select_fusion
  0.7 2.5 %sort.31 = (s32[128]{0:T(128)}, s32[128]{0:T(128)S(1)}) sort(s32[128]{0:T(128)S(1)} %and_select_fusion, s32[128]{0:T(128)S(1)} %iota.13), dimensions={0}, to_apply=%region_2.3 | sort | flops 896 | bytes 2048 | tf_op jit(solution)/shard_map/jit(argsort)/sort | solution.py:51
  3.3 0.7 gather_fusion.2
  4.0 0.7 copy.23
  4.7 11.1 %all-to-all-start.2 = ((bf16[128,1,128]{2,1,0:T(2,128)(2,1)}), bf16[128,1,128]{2,1,0:T(2,128)(2,1)S(1)}, u32[]{:S(2)}, u32[]{:S(2)}) async-start(bf16[128,1,128]{2,1,0:T(2,128)(2,1)} %copy.23), calls=%async_computation.2 | async-start | bytes 131072 | tf_op jit(solution)/shard_map/all_to_all | solution.py:56
  15.8 0.9 copy.27
  16.7 0.8 dynamic_slice.7
  17.4 5.0 %fusion.27 = (f32[16,16]{1,0:T(8,128)S(1)}, f32[16,16,2048]{2,1,0:T(8,128)S(1)}) fusion(s32[16]{0:T(128)S(1)} %dynamic_slice.7, bf16[16,16,128]{2,1,0:T(8,128)(2,1)S(1)} %bitcast.60, bf16[1,16,2048,128]{3,2,1,0:T(8,128)(2,1)} %param.8), kind=kOutput, calls=%fused_computation.45 | convolution fusion | flops 137889792 | bytes 10552384 | tf_op jit(solution)/shard_map/sub | solution.py:21
  22.5 4.7 %fusion.18 = bf16[16,16,128]{2,1,0:T(8,128)(2,1)S(1)} fusion(bf16[1,16,2048,128]{3,2,1,0:T(8,128)(2,1)} %param.9, f32[16,16,2048]{2,1,0:T(8,128)S(1)} %get-tuple-element.10, f32[16,16]{1,0:T(8,128)S(1)} %get-tuple-element.9), kind=kOutput, calls=%fused_computation.22 | convolution fusion | flops 135299072 | bytes 10552320 | tf_op jit(solution)/shard_map/rhl,rld->rhd/dot_general | solution.py:24
  27.1 0.1 reshape_reshape.3
  27.2 0.1 copy.21
  27.3 0.1 broadcast_in_dim.29
  27.4 1.0 reshape.76
  28.4 0.0 all-to-all-done.2
  28.4 9.8 %all-to-all-start = ((bf16[128,2,512]{2,1,0:T(2,128)(2,1)}), bf16[128,2,512]{2,1,0:T(2,128)(2,1)S(1)}, u32[]{:S(2)}, u32[]{:S(2)}) async-start(bf16[128,2,512]{2,1,0:T(2,128)(2,1)} %reshape.76), calls=%async_computation | async-start | bytes 524288 | tf_op jit(solution)/shard_map/all_to_all | solution.py:43
  38.1 5.2 %gather_fusion = bf16[128,128,128]{2,1,0:T(8,128)(2,1)} fusion(bf16[128,128,128]{2,1,0:T(8,128)(2,1)} %bitcast.55, s32[1024]{0:T(1024)S(1)} %pad_clamp_fusion.1), kind=kCustom, calls=%fused_computation | custom fusion | bytes 8389120 | tf_op jit(solution)/shard_map/gather | solution.py:52
  43.4 5.7 %all-to-all-done = bf16[128,2,512]{2,1,0:T(2,128)(2,1)S(1)} async-done(((bf16[128,2,512]{2,1,0:T(2,128)(2,1)}), bf16[128,2,512]{2,1,0:T(2,128)(2,1)S(1)}, u32[]{:S(2)}, u32[]{:S(2)}) %all-to-all-start) | async-done | bytes 262176 | tf_op jit(solution)/shard_map/all_to_all | solution.py:43
  49.0 5.8 %all-to-all-start.1 = ((bf16[128,128,128]{2,1,0:T(8,128)(2,1)}), bf16[128,128,128]{2,1,0:T(8,128)(2,1)}, u32[]{:S(2)}, u32[]{:S(2)}) async-start(bf16[128,128,128]{2,1,0:T(8,128)(2,1)} %gather_fusion), calls=%async_computation.1 | async-start | bytes 8388608 | tf_op jit(solution)/shard_map/all_to_all | solution.py:55
  54.9 0.1 fusion.24
  55.0 2.5 %sort.32 = (s32[128]{0:T(128)}, s32[128]{0:T(128)S(1)}) sort(s32[128]{0:T(128)S(1)} %fusion.24, s32[128]{0:T(128)S(1)} %iota.14), dimensions={0}, to_apply=%region_4.5 | sort | flops 896 | bytes 2048 | tf_op jit(solution)/shard_map/jit(argsort)/sort | solution.py:60
  57.6 0.7 gather_fusion.3
  58.3 0.1 copy.24
  58.4 0.3 reshape.77
  58.8 0.1 copy.22
  58.9 0.3 reshape.35
  59.2 48.1 %all-to-all-done.1 = bf16[128,128,128]{2,1,0:T(8,128)(2,1)} async-done(((bf16[128,128,128]{2,1,0:T(8,128)(2,1)}), bf16[128,128,128]{2,1,0:T(8,128)(2,1)}, u32[]{:S(2)}, u32[]{:S(2)}) %all-to-all-start.1) | async-done | bytes 4194336 | tf_op jit(solution)/shard_map/all_to_all | solution.py:55
  107.4 5.2 %gather_fusion.1 = bf16[128,128,128]{2,1,0:T(8,128)(2,1)} fusion(bf16[128,128,128]{2,1,0:T(8,128)(2,1)} %all-to-all-done.1, s32[1024]{0:T(1024)S(1)} %pad_clamp_fusion), kind=kCustom, calls=%fused_computation.1 | custom fusion | bytes 8389120 | tf_op jit(solution)/shard_map/gather | solution.py:61
  112.6 3.3 %convert.3 = f32[4,32,128,128]{3,2,1,0:T(8,128)S(1)} convert(bf16[4,32,128,128]{3,2,1,0:T(8,128)(2,1)} %bitcast.53) | non-fusion elementwise | flops 2097152 | bytes 12582912 | tf_op jit(solution)/shard_map/convert_element_type | solution.py:63
  115.9 11.2 %fusion.5 = bf16[4,32,128,128]{3,1,2,0:T(8,128)(2,1)S(1)} fusion(f32[4,32,128,128]{3,2,1,0:T(8,128)S(1)} %convert.3, f32[4,32,128]{1,2,0:T(8,128)S(1)} %copy.24), kind=kLoop, calls=%fused_computation.10 | loop fusion | flops 4194304 | bytes 12648448 | tf_op jit(solution)/shard_map/convert_element_type | solution.py:63
  127.1 1.7 %fusion.6 = bf16[32,8,4096]{2,1,0:T(8,128)(2,1)S(1)} fusion(bf16[256,512]{1,0:T(8,128)(2,1)S(1)} %reshape.35, bf16[64,8,32,128]{3,2,1,0:T(8,128)(2,1)S(1)} %bitcast.54), kind=kOutput, calls=%fused_computation.12 | convolution fusion | flops 1074790400 | bytes 6553600 | tf_op jit(solution)/shard_map/dot_general | solution.py:71
  128.7 32.8 %all_to_all.27 = bf16[32,8,4096]{2,1,0:T(8,128)(2,1)S(1)} all-to-all(bf16[32,8,4096]{2,1,0:T(8,128)(2,1)S(1)} %fusion.6), channel_id=1, replica_groups=mesh['grp'=4,'tp'=32] {'tp'}, dimensions={0} | all-to-all | bytes 4194304 | tf_op jit(solution)/shard_map/all_to_all | solution.py:73
  161.5 0.9 reduce_sum.32
  (11 shorter events, 0.0 us)
Async XLA Ops:
  0.0 3.3 %copy-start = (bf16[1,128,128]{2,1,0:T(8,128)(2,1)S(1)}, bf16[1,128,128]{2,1,0:T(8,128)(2,1)}, u32[]{:S(2)}) copy-start(bf16[1,128,128]{2,1,0:T(8,128)(2,1)} %param.12) | copy-start | bytes 98308
  4.7 23.7 %all-to-all-start.2 = ((bf16[128,1,128]{2,1,0:T(2,128)(2,1)}), bf16[128,1,128]{2,1,0:T(2,128)(2,1)S(1)}, u32[]{:S(2)}, u32[]{:S(2)}) async-start(bf16[128,1,128]{2,1,0:T(2,128)(2,1)} %copy.23), calls=%async_computation.2 | async-start | bytes 131072 | tf_op jit(solution)/shard_map/all_to_all | solution.py:56
  28.4 20.7 %all-to-all-start = ((bf16[128,2,512]{2,1,0:T(2,128)(2,1)}), bf16[128,2,512]{2,1,0:T(2,128)(2,1)S(1)}, u32[]{:S(2)}, u32[]{:S(2)}) async-start(bf16[128,2,512]{2,1,0:T(2,128)(2,1)} %reshape.76), calls=%async_computation | async-start | bytes 524288 | tf_op jit(solution)/shard_map/all_to_all | solution.py:43
  43.4 11.5 %copy-start.1 = (s32[128,128]{1,0:T(8,128)S(1)}, s32[128,128]{1,0:T(8,128)}, u32[]{:S(2)}) copy-start(s32[128,128]{1,0:T(8,128)} %param.13) | copy-start | bytes 196612
  49.0 58.3 %all-to-all-start.1 = ((bf16[128,128,128]{2,1,0:T(8,128)(2,1)}), bf16[128,128,128]{2,1,0:T(8,128)(2,1)}, u32[]{:S(2)}, u32[]{:S(2)}) async-start(bf16[128,128,128]{2,1,0:T(8,128)(2,1)} %gather_fusion), calls=%async_computation.1 | async-start | bytes 8388608 | tf_op jit(solution)/shard_map/all_to_all | solution.py:55

commit v2 on v1

v2 whole, which is shorter than its diff:
```python
import jax
import jax.numpy as jnp
from jax import lax
from jax.experimental import pallas as pl
from jax.experimental.pallas import tpu as pltpu
from jax.sharding import PartitionSpec as P

KV_HEADS = 8
HEAD_DIM = 128
HEADS = 16
LANES = 128
ORDERS = ("xyz", "yzx", "zxy")
COUNTS = (6, 5, 5)
STARTS = (0, 6, 11)
ROWS = 256
TILES = 128
MESH = pl.DeviceIdType.MESH


def attend_rows(queries_one, keys_one, values_one, live_len):
    row_count = queries_one.shape[0]
    per_head = queries_one.reshape(row_count, HEADS, HEAD_DIM)
    scores = jnp.einsum(
        "rhd,rld->rhl", per_head, keys_one, preferred_element_type=jnp.float32
    ) * HEAD_DIM ** (-0.5)
    inside = lax.broadcasted_iota(jnp.int32, scores.shape, 2) < live_len[:, None, None]
    scores = jnp.where(inside, scores, -1e30)
    row_max = jnp.max(scores, axis=2, keepdims=True)
    weights = jnp.where(inside, jnp.exp(scores - row_max), 0.0)
    row_sum = jnp.sum(weights, axis=2, keepdims=True)
    attn_weights = (weights / row_sum).astype(jnp.bfloat16)
    mixed_out = jnp.einsum(
        "rhl,rld->rhd", attn_weights, values_one, preferred_element_type=jnp.float32
    )
    return mixed_out.astype(jnp.bfloat16).transpose(1, 0, 2)


def tile_table(slot_tiles, grp, tp):
    core = grp % 2
    own = lax.dynamic_index_in_dim(slot_tiles, grp * 32 + tp, 0, keepdims=False)
    other = lax.dynamic_index_in_dim(
        slot_tiles, (grp + 1 - 2 * core) * 32 + tp, 0, keepdims=False
    )
    spot = lax.broadcasted_iota(jnp.int32, (TILES, TILES), 0)
    slot = lax.broadcasted_iota(jnp.int32, (TILES, TILES), 1)
    owner = ((spot // 2) % 2 * 2 + core) * 32 + spot // 4
    held = jnp.where(spot % 2 == 0, own[None], other[None])
    packed = slot * 128 + held % 128
    packed = jnp.sum(jnp.where(held // 128 == owner, packed, 0), axis=1)
    index = jnp.arange(TILES, dtype=jnp.int32)
    key = index // 2 % 2 * 32 + packed % 32
    before = (key[None] == key[:, None]) & (index[None] < index[:, None])
    previous = jnp.max(jnp.where(before, index[None], -1), axis=1)
    last = jnp.max(jnp.where(key[None] == index[:, None], index[None], -1), axis=1)
    return jnp.stack([packed // 128, packed % 128 // 32, previous, last])


def kernel(*refs):
    table, att, tiles_own, tiles_other, scales_own, scales_other, out = refs[:7]
    scratch = list(refs[7:])
    feats = [scratch.pop(0) for _ in range(3)]
    sends = [scratch.pop(0) for _ in range(3)]
    lands = [[[scratch.pop(0) for _ in range(4)] for _ in range(3)] for _ in range(3)]
    tiles, scales, weights, sums = [scratch.pop(0) for _ in range(4)]
    load_sem, ag_send, ag_recv, sib_send, sib_recv, rs_send, rs_recv = scratch

    grp, tp = lax.axis_index("grp"), lax.axis_index("tp")
    core = lax.rem(grp, 2)
    me = {"x": lax.rem(lax.div(tp, 4), 2) * 2 + lax.div(grp, 2), "y": lax.div(tp, 8), "z": lax.rem(tp, 4)}

    def shifted(axis, by):
        return lax.rem(me[axis] + by, 4)

    def device(axis, by):
        at = dict(me)
        at[axis] = shifted(axis, by)
        return (
            lax.rem(at["x"], 2) * 2 + core,
            at["y"] * 8 + lax.div(at["x"], 2) * 4 + at["z"],
        )

    nxt = {axis: device(axis, 1) for axis in "xyz"}
    prv = {axis: device(axis, 3) for axis in "xyz"}
    sibling = (grp + 1 - 2 * core, tp)

    loads = [
        pltpu.make_async_copy(tiles_own, tiles.at[0], load_sem.at[0]),
        pltpu.make_async_copy(tiles_other, tiles.at[1], load_sem.at[1]),
    ]
    for load in loads:
        load.start()

    barrier = pltpu.get_barrier_semaphore()
    for other in [*nxt.values(), *prv.values(), sibling]:
        pl.semaphore_signal(barrier, inc=1, device_id=other, device_id_type=MESH)
    pl.semaphore_wait(barrier, 7)

    def remote(src, dst, send, recv, target):
        return pltpu.make_async_remote_copy(
            src_ref=src, dst_ref=dst, send_sem=send, recv_sem=recv,
            device_id=target, device_id_type=MESH,
        )

    pending = []

    def go(copy):
        copy.start()
        pending.append(copy)
        return copy

    def halves(count, half):
        first = (count + 1) // 2
        return pl.ds(0, first) if half == 0 else pl.ds(first, count - first)

    def gather_view(p, phase, at, half):
        first, second, third = ORDERS[p]
        buf = feats[p].at[core]
        if phase == 0:
            return buf.at[me[third], me[second], at, halves(COUNTS[p], half)]
        if phase == 1:
            return buf.at[me[third], at, pl.ds(2 * half, 2)]
        return buf.at[at, pl.ds(2 * half, 2)]

    def gather_copy(p, phase, number, at, half, target):
        view = gather_view(p, phase, at, half)
        return remote(view, view, ag_send.at[p, phase, number], ag_recv.at[p, phase, number], target)

    def pass_on(p, number, view):
        go(remote(view, view, sib_send.at[p, number], sib_recv.at[p, number], sibling))

    for p in range(3):
        first, second, third = ORDERS[p]
        feats[p][core, me[third], me[second], me[first]] = att[STARTS[p] : STARTS[p] + COUNTS[p]]

    def gather_start(p, phase):
        axis = ORDERS[p][phase]
        here = me[axis]
        found = [
            go(gather_copy(p, phase, 0, here, 0, nxt[axis])),
            go(gather_copy(p, phase, 1, here, 1, prv[axis])),
            go(gather_copy(p, phase, 2, here, 1, nxt[axis])),
            go(gather_copy(p, phase, 3, here, 0, prv[axis])),
        ]
        return found

    def gather_forward(p, phase, found):
        axis = ORDERS[p][phase]
        found[0].wait_recv()
        found.append(go(gather_copy(p, phase, 4, shifted(axis, 3), 0, nxt[axis])))
        found[1].wait_recv()
        found.append(go(gather_copy(p, phase, 5, shifted(axis, 1), 1, prv[axis])))

    for phase in range(3):
        founds = []
        for p in range(3):
            founds.append(gather_start(p, phase))
        if phase == 2:
            for p in range(3):
                pass_on(p, 0, feats[p].at[core, me[ORDERS[p][2]]])
        for p in range(3):
            gather_forward(p, phase, founds[p])
            if phase == 2:
                axis = ORDERS[p][2]
                pass_on(p, 1, gather_view(p, 2, shifted(axis, 3), 0))
                pass_on(p, 2, gather_view(p, 2, shifted(axis, 1), 1))
        if phase == 2:
            for load in loads:
                load.wait()
            scales[0] = scales_own[...].astype(jnp.float32)
            scales[1] = scales_other[...].astype(jnp.float32)
            diagonal = lax.broadcasted_iota(jnp.int32, (LANES, LANES), 0) == lax.broadcasted_iota(
                jnp.int32, (LANES, LANES), 1
            )

            def dequantize(step, carry):
                for k in range(8):
                    spot = step * 8 + k
                    where = table[0, spot]
                    row = scales[k % 2, pl.ds(where, 1), :]
                    spread = jnp.where(diagonal, jnp.broadcast_to(row, (LANES, LANES)), 0.0)
                    weights[spot] = jnp.dot(
                        spread.astype(jnp.bfloat16), tiles[k % 2, where],
                        preferred_element_type=jnp.float32,
                    ).astype(jnp.bfloat16)
                return carry

            lax.fori_loop(0, TILES // 8, dequantize, 0)
        for p in range(3):
            axis = ORDERS[p][phase]
            for number in (2, 3, 4, 5):
                founds[p][number].wait_recv()
                if phase == 2:
                    by, half = ((3, 1), (1, 0), (2, 0), (2, 1))[number - 2]
                    pass_on(p, number + 1, gather_view(p, 2, shifted(axis, by), half))

    for p in range(3):
        axis = ORDERS[p][2]
        for number in range(7):
            size = feats[p].at[core, 0] if number == 0 else feats[p].at[core, 0, pl.ds(0, 2)]
            remote(size, size, sib_send.at[p, number], sib_recv.at[p, number], sibling).wait_recv()

    for p in range(3):

        def multiply(step, carry, p=p):
            for k in range(8):
                spot = (STARTS[p] + step) * 8 + k
                part = table[1, spot]
                columns = []
                for j in range(2):
                    blocks = []
                    for x_lo in range(2):
                        for c in range(2):
                            for y in range(4):
                                at = {"x": part // 2 * 2 + x_lo, "y": y, "z": part % 2 * 2 + j}
                                first, second, third = ORDERS[p]
                                blocks.append(feats[p][c, at[third], at[second], at[first], step])
                    columns.append(jnp.concatenate(blocks, axis=0))
                left = jnp.concatenate(columns, axis=1)
                weight = weights[spot]
                none = jnp.zeros((64, LANES), jnp.bfloat16)
                if k < 4:
                    weight = jnp.concatenate([weight[:64], none, weight[64:], none], axis=0)
                else:
                    weight = jnp.concatenate([none, weight[:64], none, weight[64:]], axis=0)
                term = jnp.dot(left, weight, preferred_element_type=jnp.float32)
                link = table[2, spot]
                earlier = sums[jnp.maximum(link, 0)]
                sums[spot] = term + jnp.where(link >= 0, earlier, 0.0)
            return carry

        lax.fori_loop(0, COUNTS[p], multiply, 0)

    for p in range(3):

        def lay_out(step, carry, p=p):
            for x_lo in range(2):
                pair = []
                for k in range(2):
                    link = table[3, x_lo * 32 + (STARTS[p] + step) * 2 + k]
                    pair.append(jnp.where(link >= 0, sums[jnp.maximum(link, 0)], 0.0))
                for t in range(32):
                    at = {"x": t // 4 % 2 * 2 + x_lo, "y": t // 8, "z": t % 4}
                    first, second, third = ORDERS[p]
                    unit = jnp.concatenate([half[8 * t : 8 * t + 8] for half in pair], axis=0)
                    sends[p][at[first], at[second], at[third], step] = unit.astype(jnp.bfloat16)
            return carry

        lax.fori_loop(0, COUNTS[p], lay_out, 0)

    def scatter_at(p, phase, at):
        first, second, third = ORDERS[p]
        return [(), (me[first],), (me[first], me[second])][phase] + (at,)

    def part_of(phase, count, half):
        return halves(count, half) if phase == 2 else pl.ds(2 * half, 2)

    def scatter_view(p, phase, at, half):
        return sends[p].at[scatter_at(p, phase, at) + (part_of(phase, COUNTS[p], half),)]

    def scatter_start(p, phase):
        axis = ORDERS[p][phase]
        one_r, one_l, two_r, two_l = lands[p][phase]

        def copy(number, at, half, dst, target):
            return remote(
                scatter_view(p, phase, at, half), dst,
                rs_send.at[p, phase, number], rs_recv.at[p, phase, number], target,
            )

        def two(buf, half):
            return buf.at[part_of(phase, COUNTS[p], half)]

        right, left = shifted(axis, 1), shifted(axis, 3)
        far = shifted(axis, 2)
        return [
            go(copy(0, far, 0, one_r, nxt[axis])),
            go(copy(1, far, 1, one_l, prv[axis])),
            go(copy(2, right, 1, two(two_r, 1), nxt[axis])),
            go(copy(3, left, 0, two(two_l, 0), prv[axis])),
            copy(4, right, 0, two(two_r, 0), nxt[axis]),
            copy(5, left, 1, two(two_l, 1), prv[axis]),
        ]

    def add_in(p, phase, at, half, pieces):
        base = scatter_at(p, phase, at)
        offset = 2 if half == 1 else 0
        length = 4 if half is None else 2

        def added(spots, where):
            total = sends[p][spots].astype(jnp.float32)
            for piece in pieces:
                total = total + piece[where].astype(jnp.float32)
            return total.astype(jnp.bfloat16)

        if phase == 2:
            count = COUNTS[p]
            first = (count + 1) // 2
            begin, end = (0, count) if half is None else ((0, first) if half == 0 else (first, count))
            spots = base + (slice(begin, end),)
            sends[p][spots] = added(spots, (slice(0, end - begin),))
        elif phase == 1:
            for k in range(length):
                spots = base + (offset + k,)
                sends[p][spots] = added(spots, (k,))
        else:

            def step(k, carry):
                for m in range(4):
                    spots = base + (offset + k, m)
                    sends[p][spots] = added(spots, (k, m))
                return carry

            lax.fori_loop(0, length, step, 0)

    for phase in range(3):
        copies = [scatter_start(p, phase) for p in range(3)]
        for p in range(3):
            axis = ORDERS[p][phase]
            copies[p][0].wait_recv()
            add_in(p, phase, shifted(axis, 1), 0, [lands[p][phase][0]])
            go(copies[p][4])
            copies[p][1].wait_recv()
            add_in(p, phase, shifted(axis, 3), 1, [lands[p][phase][1]])
            go(copies[p][5])
        for p in range(3):
            axis = ORDERS[p][phase]
            for number in (2, 3, 4, 5):
                copies[p][number].wait_recv()
            if phase < 2:
                add_in(p, phase, me[axis], None, lands[p][phase][2:])
            else:
                base = scatter_at(p, phase, me[axis])
                for unit in range(COUNTS[p]):
                    total = sends[p][base + (unit,)].astype(jnp.float32)
                    for piece in lands[p][phase][2:]:
                        total = total + piece[unit].astype(jnp.float32)
                    column = (STARTS[p] + unit) * 2 * LANES
                    out[:, column : column + LANES] = total[:8].astype(jnp.bfloat16)
                    out[:, column + LANES : column + 2 * LANES] = total[8:].astype(jnp.bfloat16)

    for copy in pending:
        copy.wait_send()


def scratch_shapes():
    bf16 = jnp.bfloat16
    tail = (16, LANES)
    shapes = [pltpu.VMEM((2, 4, 4, 4, n) + tail, bf16) for n in COUNTS]
    shapes += [pltpu.VMEM((4, 4, 4, n) + tail, bf16) for n in COUNTS]
    for n in COUNTS:
        for lead in ((4, 4), (4,), ()):
            if lead:
                half = half_l = (2,) + lead[1:] + (n,)
            else:
                half, half_l = ((n + 1) // 2,), (n - (n + 1) // 2,)
            full = lead + (n,)
            for dims in (half, half_l, full, full):
                shapes.append(pltpu.VMEM(dims + tail, bf16))
    shapes += [
        pltpu.VMEM((2, TILES, LANES, LANES), bf16),
        pltpu.VMEM((2, TILES, LANES), jnp.float32),
        pltpu.VMEM((TILES, LANES, LANES), bf16),
        pltpu.VMEM((TILES, ROWS, LANES), jnp.float32),
        pltpu.SemaphoreType.DMA((2,)),
        pltpu.SemaphoreType.DMA((3, 3, 6)),
        pltpu.SemaphoreType.DMA((3, 3, 6)),
        pltpu.SemaphoreType.DMA((3, 7)),
        pltpu.SemaphoreType.DMA((3, 7)),
        pltpu.SemaphoreType.DMA((3, 3, 6)),
        pltpu.SemaphoreType.DMA((3, 3, 6)),
    ]
    return shapes


def body(queries, cache_keys, cache_values, lengths, old_tiles, old_scales, slot_tiles):
    grp, tp = lax.axis_index("grp"), lax.axis_index("tp")
    swap = [(0, 1), (1, 0), (2, 3), (3, 2)]
    other_tiles = lax.ppermute(old_tiles[0], "grp", swap)
    other_scales = lax.ppermute(old_scales[0], "grp", swap)
    table = tile_table(slot_tiles, grp, tp)
    group_rows = queries.shape[1]
    first_row = (grp * 32 + tp) // KV_HEADS * group_rows
    live_len = lax.dynamic_slice_in_dim(lengths, first_row, group_rows)
    att = attend_rows(queries[0], cache_keys[0], cache_values[0], live_len)
    vmem = pl.BlockSpec(memory_space=pltpu.VMEM)
    return pl.pallas_call(
        kernel,
        out_shape=jax.ShapeDtypeStruct((8, 4096), jnp.bfloat16),
        in_specs=[
            pl.BlockSpec(memory_space=pltpu.SMEM),
            vmem,
            pl.BlockSpec(memory_space=pl.ANY),
            pl.BlockSpec(memory_space=pl.ANY),
            vmem,
            vmem,
        ],
        out_specs=vmem,
        scratch_shapes=scratch_shapes(),
        compiler_params=pltpu.CompilerParams(
            collective_id=0, has_side_effects=True, vmem_limit_bytes=58 * 2**20
        ),
    )(table, att, old_tiles[0], other_tiles, old_scales[0], other_scales)


def solution(mesh):
    return jax.shard_map(
        body,
        mesh=mesh,
        in_specs=(
            P(("grp", "tp"), None, None),
            P(("grp", "tp"), None, None, None),
            P(("grp", "tp"), None, None, None),
            P(),
            P(("grp", "tp"), None, None, None),
            P(("grp", "tp"), None, None),
            P(),
        ),
        out_specs=P("tp", "grp"),
        check_vma=False,
    )
```

time: 163 us -> 91.3 us (0.56)
  Pallas kernels: 0 us -> 74.3 us
  waiting for transfers between devices: 53.8 us -> 0.01 us
  blocking collectives: 32.8 us -> 0 us
  starting transfers between devices: 26.7 us -> 0.51 us
  other arithmetic: 21.3 us -> 1.13 us
  local copies, waits for them, and re-layouts: 16.3 us -> 5.04 us
    pallas_call x0 -> x1, Pallas kernels: none -> 74.3 us  [body(): pl.pallas_call(kernel, out_shape=jax.ShapeDtypeStruct((8, 4096), jnp.bflo...]
    all_to_all x3 -> x0, waiting for transfers between devices: 53.8 us -> none  [the longest x1 48.1 us: body(): lax.all_to_all(send_tiles, ('grp', 'tp'), split_axis=0, concat_axis=0, ti...]
    all_to_all x1 -> x0, blocking collectives: 32.8 us -> none  [body(): terms = lax.all_to_all(terms, 'tp', split_axis=0, concat_axis=0, tiled=True)]
    all_to_all x3 -> x0, starting transfers between devices: 26.7 us -> none  [the longest x1 11.1 us: body(): lax.all_to_all(send_scales, ('grp', 'tp'), split_axis=0, concat_axis=0, t...]
    convert_element_type x2 -> x0, other arithmetic: 14.4 us -> none  [the longest x1 11.2 us: body(): (placed.astype(jnp.float32) * scales.astype(jnp.float32)[:, :, None]).ast...]
    gather x4 -> x0, local copies, waits for them, and re-layouts: 11.9 us -> none  [the longest x1 5.24 us: body(): send_tiles = old_tiles[0][by_owner]]
    sort x2 -> x0, other arithmetic: 5.08 us -> none  [the longest x1 2.54 us: body(): arrange = jnp.argsort(local_index)]
    dot_general x1 -> x0, matrix products: 1.67 us -> none  [body(): product = jnp.dot(features, new_block, preferred_element_type=jnp.float32)]
  transfers between devices with their start and end apart: 3 -> 2, of which waited for: 2 -> 0; matrix products, arithmetic and copies ran while one was open for 14% -> 15% of each run, Pallas kernels for 0% -> 0%
where the time goes in v2:
time: 91.3 us; the launch traced here: 90.8 us
  Pallas kernels  74.3 us (81%)
  matrix products  9.72 us (11%)
  local copies, waits for them, and re-layouts  5.04 us (6%)
  other arithmetic  1.13 us (1%)
    pallas_call x1, Pallas kernels, body(): pl.pallas_call(kernel, out_shape=jax.ShapeDtypeStruct((8, 4096), jnp.bflo...  74.3 us
    sub x1, matrix products, attend_rows(): weights = jnp.where(inside, jnp.exp(scores - row_max), 0.0)  5.02 us
    dot_general x1, matrix products, attend_rows(): jnp.einsum('rhl,rld->rhd', attn_weights, values_one, preferred_element_ty...  4.7 us
    unnamed x4, local copies, waits for them, and re-layouts  2.92 us
  transfers between devices with their start and end apart: 2, of which 0 were waited for; matrix products, arithmetic and copies ran while one was open for 15% of the time, Pallas kernels for 0%

profile of v2, /device:TPU:0, one launch (start us, length us, event | category | flops | bytes accessed | tf_op | source)
XLA Modules:
  0.0 90.8 jit_solution(8968668625299607353)
XLA Ops:
  0.0 0.0 collective-permute-start
  0.0 0.5 collective-permute-start.1
  0.5 0.8 copy.10
  1.4 0.8 dynamic_slice.12
  2.2 0.7 dynamic-slice_bitcast_fusion.1
  2.9 0.3 fusion.24
  3.2 0.2 select_reduce_fusion.1
  3.4 5.0 %fusion.34 = (f32[16,16]{1,0:T(8,128)S(1)}, f32[16,16,2048]{2,1,0:T(8,128)S(1)}) fusion(s32[16]{0:T(128)S(1)} %dynamic_slice.12, bf16[16,16,128]{2,1,0:T(8,128)(2,1)S(1)} %bitcast.44, bf16[1,16,2048,128]{3,2,1,0:T(8,128)(2,1)} %param.8), kind=kOutput, calls=%fused_computation.82 | convolution fusion | flops 137889792 | bytes 10552384 | tf_op jit(solution)/shard_map/sub | solution.py:29
  8.5 4.7 %fusion.1 = bf16[16,16,128]{2,1,0:T(8,128)(2,1)S(1)} fusion(bf16[1,16,2048,128]{3,2,1,0:T(8,128)(2,1)} %param.9, f32[16,16,2048]{2,1,0:T(8,128)S(1)} %get-tuple-element.12, f32[16,16]{1,0:T(8,128)S(1)} %get-tuple-element.11), kind=kOutput, calls=%fused_computation.1 | convolution fusion | flops 135266304 | bytes 10552320 | tf_op jit(solution)/shard_map/rhl,rld->rhd/dot_general | solution.py:32
  13.2 0.6 pad_add_fusion.refs_0_
  13.7 0.6 copy.14
  14.4 0.0 collective-permute-done.1.refs_5_
  14.4 0.0 copy-start
  14.4 0.0 collective-permute-done.refs_3_
  14.4 0.6 copy-done
  15.0 74.3 %shard_map.73 = bf16[8,4096]{1,0:T(8,128)(2,1)} custom-call(s32[4,128]{1,0:T(4,128)} %pad_add_fusion.refs_0_, bf16[16,16,128]{2,1,0:T(8,128)(2,1)} %bitcast.45, bf16[128,128,128]{2,1,0:T(8,128)(2,1)} %bitcast.43, bf16[128,128,128]{2,1,0:T(8,128)(2,1)} %collective-permute-done.refs_3_, bf16[128,128]{1,0:T(8,128)(2,1)} %bitcast.48, bf16[128,128]{1,0:T(8,128)(2,1)} %copy-done), custom_call_target="tpu_custom_call" | custom-call | tf_op jit(solution)/shard_map/pallas_call | solution.py:386
  89.3 1.5 %copy.16 = bf16[8,4096]{1,0:T(8,128)(2,1)} copy(bf16[8,4096]{1,0:T(8,128)(2,1)} %shard_map.73) | data formatting | bytes 131072
  (8 shorter events, 0.1 us)
Async XLA Ops:
  0.0 14.4 %collective-permute-start = (bf16[128,128,128]{2,1,0:T(8,128)(2,1)}, bf16[128,128,128]{2,1,0:T(8,128)(2,1)}, u32[]{:S(2)}, u32[]{:S(2)}) collective-permute-start(bf16[128,128,128]{2,1,0:T(8,128)(2,1)} %bitcast.42), channel_id=1, source_target_pairs={{0,32},{32,0},{64,96},{96,64},{1,33},{33,1},{65,97},{97,65},{2,34}... | collective-permute-start | bytes 12582920 | tf_op jit(solution)/shard_map/ppermute | solution.py:378
  0.0 14.4 %collective-permute-start.1 = (bf16[128,128]{1,0:T(8,128)(2,1)}, bf16[128,128]{1,0:T(8,128)(2,1)S(1)}, u32[]{:S(2)}, u32[]{:S(2)}) collective-permute-start(bf16[128,128]{1,0:T(8,128)(2,1)} %bitcast.47), channel_id=1, source_target_pairs={{0,32},{32,0},{64,96},{96,64},{1,33},{33,1},{65,97},{97,65},{2,34}... | collective-permute-start | bytes 98312 | tf_op jit(solution)/shard_map/ppermute | solution.py:379
  14.4 0.6 copy-start

commit v3 on v2

v3 whole, which is shorter than its diff:
```python
import jax
import jax.numpy as jnp
from jax import lax
from jax.experimental import pallas as pl
from jax.experimental.pallas import tpu as pltpu
from jax.sharding import PartitionSpec as P

KV_HEADS = 8
HEAD_DIM = 128
HEADS = 16
LANES = 128
ORDERS = ("xyz", "yzx", "zxy")
COUNTS = (6, 5, 5)
STARTS = (0, 6, 11)
ROWS = 256
STAGE = 4
TILES = 128
MESH = pl.DeviceIdType.MESH


def tile_table(slot_tiles, grp, tp):
    core = grp % 2
    own = lax.dynamic_index_in_dim(slot_tiles, grp * 32 + tp, 0, keepdims=False)
    other = lax.dynamic_index_in_dim(
        slot_tiles, (grp + 1 - 2 * core) * 32 + tp, 0, keepdims=False
    )
    spot = lax.broadcasted_iota(jnp.int32, (TILES, TILES), 0)
    slot = lax.broadcasted_iota(jnp.int32, (TILES, TILES), 1)
    owner = ((spot // 2) % 2 * 2 + core) * 32 + spot // 4
    held = jnp.where(spot % 2 == 0, own[None], other[None])
    packed = slot * 128 + held % 128
    packed = jnp.sum(jnp.where(held // 128 == owner, packed, 0), axis=1)
    index = jnp.arange(TILES, dtype=jnp.int32)
    key = index // 2 % 2 * 32 + packed % 32
    before = (key[None] == key[:, None]) & (index[None] < index[:, None])
    previous = jnp.max(jnp.where(before, index[None], -1), axis=1)
    last = jnp.max(jnp.where(key[None] == index[:, None], index[None], -1), axis=1)
    return jnp.stack([packed // 128, packed % 128 // 32, previous, last])


def kernel(*refs):
    table, lengths, queries, keys, values, tiles_own, scales_own, out = refs[:8]
    scratch = list(refs[8:])
    feats = [scratch.pop(0) for _ in range(3)]
    sends = [scratch.pop(0) for _ in range(3)]
    lands = [[[scratch.pop(0) for _ in range(many)] for many in (4, 1, 1)] for _ in range(3)]
    tiles, scales, weights, sums = [scratch.pop(0) for _ in range(4)]
    key_buf, value_buf, att, scales_other = [scratch.pop(0) for _ in range(4)]
    kv_sem, swap_send, swap_recv = [scratch.pop(0) for _ in range(3)]
    load_sem, ag_send, ag_recv, sib_send, sib_recv, rs_send, rs_recv = scratch

    grp, tp = lax.axis_index("grp"), lax.axis_index("tp")
    core = lax.rem(grp, 2)
    me = {"x": lax.rem(lax.div(tp, 4), 2) * 2 + lax.div(grp, 2), "y": lax.div(tp, 8), "z": lax.rem(tp, 4)}

    def shifted(axis, by):
        return lax.rem(me[axis] + by, 4)

    def device(axis, by):
        at = dict(me)
        at[axis] = shifted(axis, by)
        return (
            lax.rem(at["x"], 2) * 2 + core,
            at["y"] * 8 + lax.div(at["x"], 2) * 4 + at["z"],
        )

    ring = {axis: [device(axis, by) for by in (1, 2, 3)] for axis in "xyz"}
    nxt = {axis: ring[axis][0] for axis in "xyz"}
    prv = {axis: ring[axis][2] for axis in "xyz"}
    sibling = (grp + 1 - 2 * core, tp)

    def kv_load(stage, slot):
        rows = pl.ds(stage * STAGE, STAGE)
        return [
            pltpu.make_async_copy(keys.at[rows], key_buf.at[slot], kv_sem.at[slot, 0]),
            pltpu.make_async_copy(values.at[rows], value_buf.at[slot], kv_sem.at[slot, 1]),
        ]

    for stage in range(2):
        for load in kv_load(stage, stage):
            load.start()
    loads = [pltpu.make_async_copy(tiles_own, tiles.at[0], load_sem.at[0])]
    for load in loads:
        load.start()

    barrier = pltpu.get_barrier_semaphore()
    for other in [*ring["x"], *ring["y"], *ring["z"], sibling]:
        pl.semaphore_signal(barrier, inc=1, device_id=other, device_id_type=MESH)

    def remote(src, dst, send, recv, target):
        return pltpu.make_async_remote_copy(
            src_ref=src, dst_ref=dst, send_sem=send, recv_sem=recv,
            device_id=target, device_id_type=MESH,
        )

    pending = []

    def go(copy):
        copy.start()
        pending.append(copy)
        return copy

    first_row = lax.div(grp * 32 + tp, KV_HEADS) * 16

    def attend(stage, carry):
        slot = lax.rem(stage, 2)
        for load in kv_load(stage, slot):
            load.wait()
        for k in range(STAGE):
            row = stage * STAGE + k
            scores = lax.dot_general(
                queries[row], key_buf[slot, k], (((1,), (1,)), ((), ())),
                preferred_element_type=jnp.float32,
            ) * HEAD_DIM ** (-0.5)
            inside = lax.broadcasted_iota(jnp.int32, scores.shape, 1) < lengths[first_row + row]
            scores = jnp.where(inside, scores, -1e30)
            row_max = jnp.max(scores, axis=1, keepdims=True)
            mass = jnp.where(inside, jnp.exp(scores - row_max), 0.0)
            share = 1.0 / jnp.sum(mass, axis=1, keepdims=True)
            mixed = jnp.dot(
                (mass * share).astype(jnp.bfloat16), value_buf[slot, k],
                preferred_element_type=jnp.float32,
            )
            att[:, pl.ds(row, 1), :] = mixed[:, None, :]

        @pl.when(stage < 16 // STAGE - 2)
        def _():
            for load in kv_load(stage + 2, slot):
                load.start()

        return carry

    lax.fori_loop(0, 16 // STAGE, attend, 0)
    pl.semaphore_wait(barrier, 10)
    def gather_view(p, phase, at, half):
        first, second, third = ORDERS[p]
        buf = feats[p].at[core]
        return buf.at[at, pl.ds(2 * half, 2)]

    def gather_direct(p, phase):
        first, second, third = ORDERS[p]
        axis = ORDERS[p][phase]
        buf = feats[p].at[core]
        view = buf.at[me[third], me[second], me[first]] if phase == 0 else buf.at[me[third], me[second]]
        return [
            go(remote(view, view, ag_send.at[p, phase, by], ag_recv.at[p, phase, by], ring[axis][by]))
            for by in range(3)
        ]

    def gather_copy(p, phase, number, at, half, target):
        view = gather_view(p, phase, at, half)
        return remote(view, view, ag_send.at[p, phase, number], ag_recv.at[p, phase, number], target)

    def pass_on(p, number, view):
        go(remote(view, view, sib_send.at[p, number], sib_recv.at[p, number], sibling))

    for p in range(3):
        first, second, third = ORDERS[p]
        feats[p][core, me[third], me[second], me[first]] = att[
            STARTS[p] : STARTS[p] + COUNTS[p]
        ].astype(jnp.bfloat16)

    def gather_start(p, phase):
        axis = ORDERS[p][phase]
        here = me[axis]
        found = [
            go(gather_copy(p, phase, 0, here, 0, nxt[axis])),
            go(gather_copy(p, phase, 1, here, 1, prv[axis])),
            go(gather_copy(p, phase, 2, here, 1, nxt[axis])),
            go(gather_copy(p, phase, 3, here, 0, prv[axis])),
        ]
        return found

    def gather_forward(p, phase, found):
        axis = ORDERS[p][phase]
        found[0].wait_recv()
        found.append(go(gather_copy(p, phase, 4, shifted(axis, 3), 0, nxt[axis])))
        found[1].wait_recv()
        found.append(go(gather_copy(p, phase, 5, shifted(axis, 1), 1, prv[axis])))

    for phase in range(2):
        founds = [gather_direct(p, phase) for p in range(3)]
        if phase == 0:
            swaps = [
                go(remote(tiles_own, tiles.at[1], swap_send.at[0], swap_recv.at[0], sibling)),
                go(remote(scales_own, scales_other, swap_send.at[1], swap_recv.at[1], sibling)),
            ]
        for found in founds:
            for copy in found:
                copy.wait_recv()
    phase = 2
    if phase == 2:
        founds = [gather_start(p, 2) for p in range(3)]
        for p in range(3):
            pass_on(p, 0, feats[p].at[core, me[ORDERS[p][2]]])
        for p in range(3):
            gather_forward(p, phase, founds[p])
            axis = ORDERS[p][2]
            pass_on(p, 1, gather_view(p, 2, shifted(axis, 3), 0))
            pass_on(p, 2, gather_view(p, 2, shifted(axis, 1), 1))
        if phase == 2:
            for load in loads:
                load.wait()
            for swap in swaps:
                swap.wait_recv()
            scales[0] = scales_own[...].astype(jnp.float32)
            scales[1] = scales_other[...].astype(jnp.float32)
            diagonal = lax.broadcasted_iota(jnp.int32, (LANES, LANES), 0) == lax.broadcasted_iota(
                jnp.int32, (LANES, LANES), 1
            )

            def dequantize(step, carry):
                for k in range(8):
                    spot = step * 8 + k
                    where = table[0, spot]
                    row = scales[k % 2, pl.ds(where, 1), :]
                    spread = jnp.where(diagonal, jnp.broadcast_to(row, (LANES, LANES)), 0.0)
                    weights[spot] = jnp.dot(
                        spread.astype(jnp.bfloat16), tiles[k % 2, where],
                        preferred_element_type=jnp.float32,
                    ).astype(jnp.bfloat16)
                return carry

            lax.fori_loop(0, TILES // 8, dequantize, 0)
        for p in range(3):
            axis = ORDERS[p][phase]
            for number in (2, 3, 4, 5):
                founds[p][number].wait_recv()
                if phase == 2:
                    by, half = ((3, 1), (1, 0), (2, 0), (2, 1))[number - 2]
                    pass_on(p, number + 1, gather_view(p, 2, shifted(axis, by), half))

    for p in range(3):
        axis = ORDERS[p][2]
        for number in range(7):
            size = feats[p].at[core, 0] if number == 0 else feats[p].at[core, 0, pl.ds(0, 2)]
            remote(size, size, sib_send.at[p, number], sib_recv.at[p, number], sibling).wait_recv()

    for p in range(3):

        def multiply(step, carry, p=p):
            for k in range(8):
                spot = (STARTS[p] + step) * 8 + k
                part = table[1, spot]
                columns = []
                for j in range(2):
                    blocks = []
                    for x_lo in range(2):
                        for c in range(2):
                            for y in range(4):
                                at = {"x": part // 2 * 2 + x_lo, "y": y, "z": part % 2 * 2 + j}
                                first, second, third = ORDERS[p]
                                blocks.append(feats[p][c, at[third], at[second], at[first], step])
                    columns.append(jnp.concatenate(blocks, axis=0))
                left = jnp.concatenate(columns, axis=1)
                weight = weights[spot]
                none = jnp.zeros((64, LANES), jnp.bfloat16)
                if k < 4:
                    weight = jnp.concatenate([weight[:64], none, weight[64:], none], axis=0)
                else:
                    weight = jnp.concatenate([none, weight[:64], none, weight[64:]], axis=0)
                term = jnp.dot(left, weight, preferred_element_type=jnp.float32)
                link = table[2, spot]
                earlier = sums[jnp.maximum(link, 0)]
                sums[spot] = term + jnp.where(link >= 0, earlier, 0.0)
            return carry

        lax.fori_loop(0, COUNTS[p], multiply, 0)

    def scatter_start(p):
        axis = ORDERS[p][0]
        one_r, one_l, two_r, two_l = lands[p][0]

        def half_of(buf, half):
            return buf.at[pl.ds(2 * half, 2)]

        def copy(number, at, half, dst, target):
            return remote(
                half_of(sends[p].at[at], half), dst,
                rs_send.at[p, 0, number], rs_recv.at[p, 0, number], target,
            )

        right, left = shifted(axis, 1), shifted(axis, 3)
        far = shifted(axis, 2)
        return [
            go(copy(0, far, 0, one_r, nxt[axis])),
            go(copy(1, far, 1, one_l, prv[axis])),
            go(copy(2, right, 1, half_of(two_r, 1), nxt[axis])),
            go(copy(3, left, 0, half_of(two_l, 0), prv[axis])),
            copy(4, right, 0, half_of(two_r, 0), nxt[axis]),
            copy(5, left, 1, half_of(two_l, 1), prv[axis]),
        ]

    def scatter_direct(p, phase):
        axis = ORDERS[p][phase]
        first, second, third = ORDERS[p]
        base = (me[first],) if phase == 1 else (me[first], me[second])
        return [
            go(
                remote(
                    sends[p].at[base + (shifted(axis, by + 1),)], lands[p][phase][0].at[by],
                    rs_send.at[p, phase, by], rs_recv.at[p, phase, by], ring[axis][by],
                )
            )
            for by in range(3)
        ]

    def add_in(p, at, half, pieces):
        offset = 2 if half == 1 else 0

        def step(k, carry):
            for m in range(4):
                total = sends[p][at, offset + k, m].astype(jnp.float32)
                for piece in pieces:
                    total = total + piece[k, m].astype(jnp.float32)
                sends[p][at, offset + k, m] = total.astype(jnp.bfloat16)
            return carry

        lax.fori_loop(0, 4 if half is None else 2, step, 0)

    copies = []
    for p in range(3):

        def lay_out(step, carry, p=p):
            for x_lo in range(2):
                pair = []
                for k in range(2):
                    link = table[3, x_lo * 32 + (STARTS[p] + step) * 2 + k]
                    pair.append(jnp.where(link >= 0, sums[jnp.maximum(link, 0)], 0.0))
                for t in range(32):
                    at = {"x": t // 4 % 2 * 2 + x_lo, "y": t // 8, "z": t % 4}
                    first, second, third = ORDERS[p]
                    unit = jnp.concatenate([half[8 * t : 8 * t + 8] for half in pair], axis=0)
                    sends[p][at[first], at[second], at[third], step] = unit.astype(jnp.bfloat16)
            return carry

        lax.fori_loop(0, COUNTS[p], lay_out, 0)
        copies.append(scatter_start(p))

    for p in range(3):
        axis = ORDERS[p][0]
        copies[p][0].wait_recv()
        add_in(p, shifted(axis, 1), 0, [lands[p][0][0]])
        go(copies[p][4])
        copies[p][1].wait_recv()
        add_in(p, shifted(axis, 3), 1, [lands[p][0][1]])
        go(copies[p][5])
    direct = []
    for p in range(3):
        for number in (2, 3, 4, 5):
            copies[p][number].wait_recv()
        add_in(p, me[ORDERS[p][0]], None, lands[p][0][2:])
        direct.append(scatter_direct(p, 1))
    last = []
    for p in range(3):
        for copy in direct[p]:
            copy.wait_recv()
        base = (me[ORDERS[p][0]], me[ORDERS[p][1]])
        for k in range(4):
            total = sends[p][base + (k,)].astype(jnp.float32)
            for by in range(3):
                total = total + lands[p][1][0][by, k].astype(jnp.float32)
            sends[p][base + (k,)] = total.astype(jnp.bfloat16)
        last.append(scatter_direct(p, 2))
    for p in range(3):
        for copy in last[p]:
            copy.wait_recv()
        base = (me[ORDERS[p][0]], me[ORDERS[p][1]], me[ORDERS[p][2]])
        for unit in range(COUNTS[p]):
            total = sends[p][base + (unit,)].astype(jnp.float32)
            for by in range(3):
                total = total + lands[p][2][0][by, unit].astype(jnp.float32)
            column = (STARTS[p] + unit) * 2 * LANES
            out[:, column : column + LANES] = total[:8].astype(jnp.bfloat16)
            out[:, column + LANES : column + 2 * LANES] = total[8:].astype(jnp.bfloat16)

    for copy in pending:
        copy.wait_send()


def scratch_shapes():
    bf16 = jnp.bfloat16
    tail = (16, LANES)
    shapes = [pltpu.VMEM((2, 4, 4, 4, n) + tail, bf16) for n in COUNTS]
    shapes += [pltpu.VMEM((4, 4, 4, n) + tail, bf16) for n in COUNTS]
    for n in COUNTS:
        shapes += [pltpu.VMEM((2, 4, n) + tail, bf16)] * 2 + [pltpu.VMEM((4, 4, n) + tail, bf16)] * 2
        shapes += [pltpu.VMEM((3, 4, n) + tail, bf16), pltpu.VMEM((3, n) + tail, bf16)]
    shapes += [
        pltpu.VMEM((2, TILES, LANES, LANES), bf16),
        pltpu.VMEM((2, TILES, LANES), jnp.float32),
        pltpu.VMEM((TILES, LANES, LANES), bf16),
        pltpu.VMEM((TILES, ROWS, LANES), jnp.float32),
        pltpu.VMEM((2, STAGE, 2048, LANES), bf16),
        pltpu.VMEM((2, STAGE, 2048, LANES), bf16),
        pltpu.VMEM((HEADS, 16, LANES), jnp.float32),
        pltpu.VMEM((TILES, LANES), bf16),
        pltpu.SemaphoreType.DMA((2, 2)),
        pltpu.SemaphoreType.DMA((2,)),
        pltpu.SemaphoreType.DMA((2,)),
        pltpu.SemaphoreType.DMA((1,)),
        pltpu.SemaphoreType.DMA((3, 3, 6)),
        pltpu.SemaphoreType.DMA((3, 3, 6)),
        pltpu.SemaphoreType.DMA((3, 7)),
        pltpu.SemaphoreType.DMA((3, 7)),
        pltpu.SemaphoreType.DMA((3, 3, 6)),
        pltpu.SemaphoreType.DMA((3, 3, 6)),
    ]
    return shapes


def body(queries, cache_keys, cache_values, lengths, old_tiles, old_scales, slot_tiles):
    grp, tp = lax.axis_index("grp"), lax.axis_index("tp")
    table = tile_table(slot_tiles, grp, tp)
    vmem = pl.BlockSpec(memory_space=pltpu.VMEM)
    return pl.pallas_call(
        kernel,
        out_shape=jax.ShapeDtypeStruct((8, 4096), jnp.bfloat16),
        in_specs=[
            pl.BlockSpec(memory_space=pltpu.SMEM),
            pl.BlockSpec(memory_space=pltpu.SMEM),
            vmem,
            pl.BlockSpec(memory_space=pl.ANY),
            pl.BlockSpec(memory_space=pl.ANY),
            pl.BlockSpec(memory_space=pl.ANY),
            vmem,
        ],
        out_specs=vmem,
        scratch_shapes=scratch_shapes(),
        compiler_params=pltpu.CompilerParams(
            collective_id=0, has_side_effects=True, vmem_limit_bytes=58 * 2**20
        ),
    )(
        table, lengths, queries.reshape(16, HEADS, HEAD_DIM), cache_keys[0], cache_values[0],
        old_tiles[0], old_scales[0],
    )


def solution(mesh):
    return jax.shard_map(
        body,
        mesh=mesh,
        in_specs=(
            P(("grp", "tp"), None, None),
            P(("grp", "tp"), None, None, None),
            P(("grp", "tp"), None, None, None),
            P(),
            P(("grp", "tp"), None, None, None),
            P(("grp", "tp"), None, None),
            P(),
        ),
        out_specs=P("tp", "grp"),
        check_vma=False,
    )
```

time: 91.3 us -> 84.6 us (0.927)
  matrix products: 9.72 us -> 0 us
  Pallas kernels: 74.3 us -> 79.3 us
  local copies, waits for them, and re-layouts: 5.04 us -> 3.66 us
    sub x1 -> x0, matrix products: 5.02 us -> none  [attend_rows(): weights = jnp.where(inside, jnp.exp(scores - row_max), 0.0)]
    pallas_call x1, Pallas kernels: 74.3 us -> 79.3 us  [body(): pl.pallas_call(kernel, out_shape=jax.ShapeDtypeStruct((8, 4096), jnp.bflo...]
    dot_general x1 -> x0, matrix products: 4.7 us -> none  [attend_rows(): jnp.einsum('rhl,rld->rhd', attn_weights, values_one, preferred_element_ty...]
    unnamed x4 -> x2, local copies, waits for them, and re-layouts: 2.92 us -> 2.95 us
  transfers between devices with their start and end apart: 2 -> 0, of which waited for: 0 -> 0; matrix products, arithmetic and copies ran while one was open for 15% -> 0% of each run, Pallas kernels for 0% -> 0%
where the time goes in v3:
time: 84.6 us; the launch traced here: 84.1 us
  Pallas kernels  79.3 us (94%)
  local copies, waits for them, and re-layouts  3.66 us (4%)
  other arithmetic  1.12 us (1%)
    pallas_call x1, Pallas kernels, body(): pl.pallas_call(kernel, out_shape=jax.ShapeDtypeStruct((8, 4096), jnp.bflo...  79.3 us
    unnamed x2, local copies, waits for them, and re-layouts  2.95 us

profile of v3, /device:TPU:0, one launch (start us, length us, event | category | flops | bytes accessed | tf_op | source)
XLA Modules:
  0.0 84.1 jit_solution(15408059851606108976)
XLA Ops:
  0.0 0.7 dynamic-slice_bitcast_fusion.1
  0.8 0.3 fusion.9
  1.1 0.2 select_reduce_fusion.1
  1.3 0.6 pad_add_fusion.refs_0_
  1.9 1.5 %copy.8 = bf16[2,8,16,128]{3,2,1,0:T(8,128)(2,1)} copy(bf16[2,8,16,128]{3,1,2,0:T(8,128)(2,1)} %bitcast.32) | data formatting | bytes 131072
  3.3 79.3 %shard_map.73 = bf16[8,4096]{1,0:T(8,128)(2,1)} custom-call(s32[4,128]{1,0:T(4,128)} %pad_add_fusion.refs_0_, s32[256]{0:T(256)} %refs_1_.1, bf16[16,16,128]{2,1,0:T(8,128)(2,1)} %bitcast.31, bf16[16,2048,128]{2,1,0:T(8,128)(2,1)} %bitcast.28, bf16[16,2048,128]{2,1,0:T(8,128)(2,1)} %bitcast.29, bf16[128,128,128]{2,1,0:T(8,128)(2,1)} %bitcast.30, ...), custom_call_target="tpu_custom_call" | custom-call | tf_op jit(solution)/shard_map/pallas_call | solution.py:416
  82.6 1.5 %copy.10 = bf16[8,4096]{1,0:T(8,128)(2,1)} copy(bf16[8,4096]{1,0:T(8,128)(2,1)} %shard_map.73) | data formatting | bytes 131072
  (8 shorter events, 0.1 us)

commit v4 on v3

v4 whole, which is shorter than its diff:
```python
import jax
import jax.numpy as jnp
from jax import lax
from jax.experimental import pallas as pl
from jax.experimental.pallas import tpu as pltpu
from jax.sharding import PartitionSpec as P

KV_HEADS = 8
HEAD_DIM = 128
HEADS = 16
LANES = 128
ORDERS = ("xyz", "yzx", "zxy")
COUNTS = (6, 5, 5)
STARTS = (0, 6, 11)
ROWS = 256
STAGE = 4
TILES = 128
MESH = pl.DeviceIdType.MESH


def tile_table(slot_tiles, grp, tp):
    core = grp % 2
    own = lax.dynamic_index_in_dim(slot_tiles, grp * 32 + tp, 0, keepdims=False)
    other = lax.dynamic_index_in_dim(
        slot_tiles, (grp + 1 - 2 * core) * 32 + tp, 0, keepdims=False
    )
    spot = lax.broadcasted_iota(jnp.int32, (TILES, TILES), 0)
    slot = lax.broadcasted_iota(jnp.int32, (TILES, TILES), 1)
    owner = ((spot // 2) % 2 * 2 + core) * 32 + spot // 4
    held = jnp.where(spot % 2 == 0, own[None], other[None])
    packed = slot * 128 + held % 128
    packed = jnp.sum(jnp.where(held // 128 == owner, packed, 0), axis=1)
    index = jnp.arange(TILES, dtype=jnp.int32)
    key = index // 2 % 2 * 32 + packed % 32
    before = (key[None] == key[:, None]) & (index[None] < index[:, None])
    previous = jnp.max(jnp.where(before, index[None], -1), axis=1)
    last = jnp.max(jnp.where(key[None] == index[:, None], index[None], -1), axis=1)
    return jnp.stack([packed // 128, packed % 128 // 32, previous, last])


def order_of(p, core):
    return ORDERS[(p + core) % 3]


def kernel(*refs):
    table, lengths, queries, keys, values, tiles_own, scales_own, out = refs[:8]
    scratch = list(refs[8:])
    feats = [scratch.pop(0) for _ in range(3)]
    sends = [scratch.pop(0) for _ in range(3)]
    lands = [[[scratch.pop(0) for _ in range(many)] for many in (4, 1, 1)] for _ in range(3)]
    tiles, scales, weights, sums = [scratch.pop(0) for _ in range(4)]
    key_buf, value_buf, att, scales_other, by_row = [scratch.pop(0) for _ in range(5)]
    kv_sem, swap_send, swap_recv = [scratch.pop(0) for _ in range(3)]
    load_sem, ag_send, ag_recv, sib_send, sib_recv, rs_send, rs_recv = scratch

    grp, tp = lax.axis_index("grp"), lax.axis_index("tp")
    core = lax.rem(grp, 2)
    me = {"x": lax.rem(lax.div(tp, 4), 2) * 2 + lax.div(grp, 2), "y": lax.div(tp, 8), "z": lax.rem(tp, 4)}

    def shifted(axis, by):
        return lax.rem(me[axis] + by, 4)

    def device(axis, by):
        at = dict(me)
        at[axis] = shifted(axis, by)
        return (
            lax.rem(at["x"], 2) * 2 + core,
            at["y"] * 8 + lax.div(at["x"], 2) * 4 + at["z"],
        )

    ring = {axis: [device(axis, by) for by in (1, 2, 3)] for axis in "xyz"}

    def either(a, b):
        return jnp.where(core == 0, a, b)

    spots, rings = [], []
    for p in range(3):
        mine = list(zip(order_of(p, 0), order_of(p, 1)))
        spots.append([either(me[a], me[b]) for a, b in mine])
        rings.append(
            [[tuple(map(either, ring[a][by], ring[b][by])) for by in range(3)] for a, b in mine]
        )

    def moved(p, phase, by):
        return lax.rem(spots[p][phase] + by, 4)

    sibling = (grp + 1 - 2 * core, tp)

    def kv_load(stage, slot):
        rows = pl.ds(stage * STAGE, STAGE)
        return [
            pltpu.make_async_copy(keys.at[rows], key_buf.at[slot], kv_sem.at[slot, 0]),
            pltpu.make_async_copy(values.at[rows], value_buf.at[slot], kv_sem.at[slot, 1]),
        ]

    for stage in range(2):
        for load in kv_load(stage, stage):
            load.start()
    loads = [pltpu.make_async_copy(tiles_own, tiles.at[0], load_sem.at[0])]

    barrier = pltpu.get_barrier_semaphore()
    for other in [*ring["x"], *ring["y"], *ring["z"], sibling]:
        pl.semaphore_signal(barrier, inc=1, device_id=other, device_id_type=MESH)

    def remote(src, dst, send, recv, target):
        return pltpu.make_async_remote_copy(
            src_ref=src, dst_ref=dst, send_sem=send, recv_sem=recv,
            device_id=target, device_id_type=MESH,
        )

    pending = []

    def go(copy):
        copy.start()
        pending.append(copy)
        return copy

    for h in range(HEADS):
        head = queries[:, h * HEAD_DIM : (h + 1) * HEAD_DIM].astype(jnp.float32)
        by_row[:, h : h + 1, :] = head[:, None, :]
    first_row = lax.div(grp * 32 + tp, KV_HEADS) * 16

    def attend(stage, carry):
        slot = lax.rem(stage, 2)
        for load in kv_load(stage, slot):
            load.wait()
        live, masses = [], []
        for k in range(STAGE):
            row = stage * STAGE + k
            scores = lax.dot_general(
                by_row[row].astype(jnp.bfloat16), key_buf[slot, k], (((1,), (1,)), ((), ())),
                preferred_element_type=jnp.float32,
            ) * HEAD_DIM ** (-0.5)
            live.append(scores)
        for k in range(STAGE):
            row = stage * STAGE + k
            inside = lax.broadcasted_iota(jnp.int32, live[k].shape, 1) < lengths[first_row + row]
            scores = jnp.where(inside, live[k], -1e30)
            row_max = jnp.max(scores, axis=1, keepdims=True)
            mass = jnp.where(inside, jnp.exp(scores - row_max), 0.0)
            share = 1.0 / jnp.sum(mass, axis=1, keepdims=True)
            masses.append((mass * share).astype(jnp.bfloat16))
        for k in range(STAGE):
            row = stage * STAGE + k
            mixed = jnp.dot(masses[k], value_buf[slot, k], preferred_element_type=jnp.float32)
            att[:, pl.ds(row, 1), :] = mixed[:, None, :]

        @pl.when(stage < 16 // STAGE - 2)
        def _():
            for load in kv_load(stage + 2, slot):
                load.start()

        return carry

    lax.fori_loop(0, 16 // STAGE, attend, 0)
    for load in loads:
        load.start()
    pl.semaphore_wait(barrier, 10)
    def gather_view(p, at, half):
        return feats[p].at[core, at, pl.ds(2 * half, 2)]

    def gather_direct(p, phase):
        first, second, third = spots[p]
        view = feats[p].at[core, third, second, first] if phase == 0 else feats[p].at[core, third, second]
        return [
            go(remote(view, view, ag_send.at[p, phase, by], ag_recv.at[p, phase, by], rings[p][phase][by]))
            for by in range(3)
        ]

    def gather_copy(p, number, at, half, target):
        view = gather_view(p, at, half)
        return go(remote(view, view, ag_send.at[p, 2, number], ag_recv.at[p, 2, number], target))

    def pass_on(p, number, view):
        go(remote(view, view, sib_send.at[p, number], sib_recv.at[p, number], sibling))

    def gather_start(p):
        here = spots[p][2]
        nxt, prv = rings[p][2][0], rings[p][2][2]
        return [
            gather_copy(p, 0, here, 0, nxt),
            gather_copy(p, 1, here, 1, prv),
            gather_copy(p, 2, here, 1, nxt),
            gather_copy(p, 3, here, 0, prv),
        ]

    def gather_forward(p, found):
        nxt, prv = rings[p][2][0], rings[p][2][2]
        found[0].wait_recv()
        found.append(gather_copy(p, 4, moved(p, 2, 3), 0, nxt))
        found[1].wait_recv()
        found.append(gather_copy(p, 5, moved(p, 2, 1), 1, prv))

    begun = []
    for p in range(3):
        first, second, third = spots[p]
        feats[p][core, third, second, first] = att[STARTS[p] : STARTS[p] + COUNTS[p]].astype(jnp.bfloat16)
        begun.append(gather_direct(p, 0))
    swaps = [
        go(remote(tiles_own, tiles.at[1], swap_send.at[0], swap_recv.at[0], sibling)),
        go(remote(scales_own, scales_other, swap_send.at[1], swap_recv.at[1], sibling)),
    ]
    across = []
    for p in range(3):
        for copy in begun[p]:
            copy.wait_recv()
        across.append(gather_direct(p, 1))
    founds = []
    for p in range(3):
        for copy in across[p]:
            copy.wait_recv()
        founds.append(gather_start(p))
        pass_on(p, 0, feats[p].at[core, spots[p][2]])
    for p in range(3):
        gather_forward(p, founds[p])
        pass_on(p, 1, gather_view(p, moved(p, 2, 3), 0))
        pass_on(p, 2, gather_view(p, moved(p, 2, 1), 1))
    for load in loads:
        load.wait()
    for swap in swaps:
        swap.wait_recv()
    scales[0] = scales_own[...].astype(jnp.float32)
    scales[1] = scales_other[...].astype(jnp.float32)
    diagonal = lax.broadcasted_iota(jnp.int32, (LANES, LANES), 0) == lax.broadcasted_iota(
        jnp.int32, (LANES, LANES), 1
    )

    def dequantize(step, carry):
        for k in range(8):
            spot = step * 8 + k
            where = table[0, spot]
            row = scales[k % 2, pl.ds(where, 1), :]
            spread = jnp.where(diagonal, jnp.broadcast_to(row, (LANES, LANES)), 0.0)
            weights[spot] = jnp.dot(
                spread.astype(jnp.bfloat16), tiles[k % 2, where],
                preferred_element_type=jnp.float32,
            ).astype(jnp.bfloat16)
        return carry

    lax.fori_loop(0, TILES // 8, dequantize, 0)
    for p in range(3):
        for number in (2, 3, 4, 5):
            founds[p][number].wait_recv()
            by, half = ((3, 1), (1, 0), (2, 0), (2, 1))[number - 2]
            pass_on(p, number + 1, gather_view(p, moved(p, 2, by), half))

    for p in range(3):
        for number in range(7):
            size = feats[p].at[core, 0] if number == 0 else feats[p].at[core, 0, pl.ds(0, 2)]
            remote(size, size, sib_send.at[p, number], sib_recv.at[p, number], sibling).wait_recv()

    for p in range(3):

        def multiply(step, carry, p=p):
            for k in range(8):
                spot = (STARTS[p] + step) * 8 + k
                part = table[1, spot]
                columns = []
                for j in range(2):
                    blocks = []
                    for x_lo in range(2):
                        for c in range(2):
                            for y in range(4):
                                at = {"x": part // 2 * 2 + x_lo, "y": y, "z": part % 2 * 2 + j}
                                first, second, third = order_of(p, c)
                                blocks.append(feats[p][c, at[third], at[second], at[first], step])
                    columns.append(jnp.concatenate(blocks, axis=0))
                left = jnp.concatenate(columns, axis=1)
                weight = weights[spot]
                none = jnp.zeros((64, LANES), jnp.bfloat16)
                if k < 4:
                    weight = jnp.concatenate([weight[:64], none, weight[64:], none], axis=0)
                else:
                    weight = jnp.concatenate([none, weight[:64], none, weight[64:]], axis=0)
                term = jnp.dot(left, weight, preferred_element_type=jnp.float32)
                link = table[2, spot]
                earlier = sums[jnp.maximum(link, 0)]
                sums[spot] = term + jnp.where(link >= 0, earlier, 0.0)
            return carry

        lax.fori_loop(0, COUNTS[p], multiply, 0)

    def scatter_start(p):
        nxt, prv = rings[p][0][0], rings[p][0][2]
        one_r, one_l, two_r, two_l = lands[p][0]

        def half_of(buf, half):
            return buf.at[pl.ds(2 * half, 2)]

        def copy(number, at, half, dst, target):
            return remote(
                half_of(sends[p].at[at], half), dst,
                rs_send.at[p, 0, number], rs_recv.at[p, 0, number], target,
            )

        right, far, left = (moved(p, 0, by) for by in (1, 2, 3))
        return [
            go(copy(0, far, 0, one_r, nxt)),
            go(copy(1, far, 1, one_l, prv)),
            go(copy(2, right, 1, half_of(two_r, 1), nxt)),
            go(copy(3, left, 0, half_of(two_l, 0), prv)),
            copy(4, right, 0, half_of(two_r, 0), nxt),
            copy(5, left, 1, half_of(two_l, 1), prv),
        ]

    def scatter_direct(p, phase):
        base = tuple(spots[p][:phase])
        return [
            go(
                remote(
                    sends[p].at[base + (moved(p, phase, by + 1),)], lands[p][phase][0].at[by],
                    rs_send.at[p, phase, by], rs_recv.at[p, phase, by], rings[p][phase][by],
                )
            )
            for by in range(3)
        ]

    def add_in(p, at, half, pieces):
        offset = 2 if half == 1 else 0

        def step(k, carry):
            for m in range(4):
                total = sends[p][at, offset + k, m].astype(jnp.float32)
                for piece in pieces:
                    total = total + piece[k, m].astype(jnp.float32)
                sends[p][at, offset + k, m] = total.astype(jnp.bfloat16)
            return carry

        lax.fori_loop(0, 4 if half is None else 2, step, 0)

    copies = []
    for p in range(3):

        def lay_out(step, carry, p=p):
            for x_lo in range(2):
                pair = []
                for k in range(2):
                    link = table[3, x_lo * 32 + (STARTS[p] + step) * 2 + k]
                    pair.append(jnp.where(link >= 0, sums[jnp.maximum(link, 0)], 0.0))
                for t in range(32):
                    at = {"x": t // 4 % 2 * 2 + x_lo, "y": t // 8, "z": t % 4}
                    zero, one = order_of(p, 0), order_of(p, 1)
                    first, second, third = (either(at[a], at[b]) for a, b in zip(zero, one))
                    unit = jnp.concatenate([half[8 * t : 8 * t + 8] for half in pair], axis=0)
                    sends[p][first, second, third, step] = unit.astype(jnp.bfloat16)
            return carry

        lax.fori_loop(0, COUNTS[p], lay_out, 0)
        copies.append(scatter_start(p))

    for p in range(3):
        copies[p][0].wait_recv()
        add_in(p, moved(p, 0, 1), 0, [lands[p][0][0]])
        go(copies[p][4])
        copies[p][1].wait_recv()
        add_in(p, moved(p, 0, 3), 1, [lands[p][0][1]])
        go(copies[p][5])
    direct = []
    for p in range(3):
        for number in (2, 3, 4, 5):
            copies[p][number].wait_recv()
        add_in(p, spots[p][0], None, lands[p][0][2:])
        direct.append(scatter_direct(p, 1))
    last = []
    for p in range(3):
        for copy in direct[p]:
            copy.wait_recv()
        base = tuple(spots[p][:2])
        for k in range(4):
            total = sends[p][base + (k,)].astype(jnp.float32)
            for by in range(3):
                total = total + lands[p][1][0][by, k].astype(jnp.float32)
            sends[p][base + (k,)] = total.astype(jnp.bfloat16)
        last.append(scatter_direct(p, 2))
    for p in range(3):
        for copy in last[p]:
            copy.wait_recv()
        base = tuple(spots[p])
        for unit in range(COUNTS[p]):
            total = sends[p][base + (unit,)].astype(jnp.float32)
            for by in range(3):
                total = total + lands[p][2][0][by, unit].astype(jnp.float32)
            column = (STARTS[p] + unit) * 2 * LANES
            out[:, column : column + LANES] = total[:8]
            out[:, column + LANES : column + 2 * LANES] = total[8:]

    for copy in pending:
        copy.wait_send()


def scratch_shapes():
    bf16 = jnp.bfloat16
    tail = (16, LANES)
    shapes = [pltpu.VMEM((2, 4, 4, 4, n) + tail, bf16) for n in COUNTS]
    shapes += [pltpu.VMEM((4, 4, 4, n) + tail, bf16) for n in COUNTS]
    for n in COUNTS:
        shapes += [pltpu.VMEM((2, 4, n) + tail, bf16)] * 2 + [pltpu.VMEM((4, 4, n) + tail, bf16)] * 2
        shapes += [pltpu.VMEM((3, 4, n) + tail, bf16), pltpu.VMEM((3, n) + tail, bf16)]
    shapes += [
        pltpu.VMEM((2, TILES, LANES, LANES), bf16),
        pltpu.VMEM((2, TILES, LANES), jnp.float32),
        pltpu.VMEM((TILES, LANES, LANES), bf16),
        pltpu.VMEM((TILES, ROWS, LANES), jnp.float32),
        pltpu.VMEM((2, STAGE, 2048, LANES), bf16),
        pltpu.VMEM((2, STAGE, 2048, LANES), bf16),
        pltpu.VMEM((HEADS, 16, LANES), jnp.float32),
        pltpu.VMEM((TILES, LANES), bf16),
        pltpu.VMEM((16, HEADS, LANES), jnp.float32),
        pltpu.SemaphoreType.DMA((2, 2)),
        pltpu.SemaphoreType.DMA((2,)),
        pltpu.SemaphoreType.DMA((2,)),
        pltpu.SemaphoreType.DMA((1,)),
        pltpu.SemaphoreType.DMA((3, 3, 6)),
        pltpu.SemaphoreType.DMA((3, 3, 6)),
        pltpu.SemaphoreType.DMA((3, 7)),
        pltpu.SemaphoreType.DMA((3, 7)),
        pltpu.SemaphoreType.DMA((3, 3, 6)),
        pltpu.SemaphoreType.DMA((3, 3, 6)),
    ]
    return shapes


def body(queries, cache_keys, cache_values, lengths, old_tiles, old_scales, slot_tiles):
    grp, tp = lax.axis_index("grp"), lax.axis_index("tp")
    table = tile_table(slot_tiles, grp, tp)
    vmem = pl.BlockSpec(memory_space=pltpu.VMEM)
    result = pl.pallas_call(
        kernel,
        out_shape=jax.ShapeDtypeStruct((8, 4096), jnp.float32),
        in_specs=[
            pl.BlockSpec(memory_space=pltpu.SMEM),
            pl.BlockSpec(memory_space=pltpu.SMEM),
            vmem,
            pl.BlockSpec(memory_space=pl.ANY),
            pl.BlockSpec(memory_space=pl.ANY),
            pl.BlockSpec(memory_space=pl.ANY),
            vmem,
        ],
        out_specs=vmem,
        scratch_shapes=scratch_shapes(),
        compiler_params=pltpu.CompilerParams(
            collective_id=0, has_side_effects=True, vmem_limit_bytes=58 * 2**20
        ),
    )(
        table, lengths, queries[0], cache_keys[0], cache_values[0],
        old_tiles[0], old_scales[0],
    )
    return result.astype(jnp.bfloat16)


def solution(mesh):
    return jax.shard_map(
        body,
        mesh=mesh,
        in_specs=(
            P(("grp", "tp"), None, None),
            P(("grp", "tp"), None, None, None),
            P(("grp", "tp"), None, None, None),
            P(),
            P(("grp", "tp"), None, None, None),
            P(("grp", "tp"), None, None),
            P(),
        ),
        out_specs=P("tp", "grp"),
        check_vma=False,
    )
```

time: 84.6 us -> 78 us (0.922)
  Pallas kernels: 79.3 us -> 73.9 us
  local copies, waits for them, and re-layouts: 3.66 us -> 0.71 us
  other arithmetic: 1.12 us -> 2.68 us
    pallas_call x1, Pallas kernels: 79.3 us -> 73.9 us  [body(): pl.pallas_call(kernel, out_shape=jax.ShapeDtypeStruct((8, 4096), jnp.floa...]
    unnamed x2 -> x0, local copies, waits for them, and re-layouts: 2.95 us -> none
    convert_element_type x0 -> x1, other arithmetic: none -> 1.54 us  [body(): return result.astype(jnp.bfloat16)]
where the time goes in v4:
time: 78 us; the launch traced here: 77.3 us
  Pallas kernels  73.9 us (95%)
  other arithmetic  2.68 us (3%)
    pallas_call x1, Pallas kernels, body(): pl.pallas_call(kernel, out_shape=jax.ShapeDtypeStruct((8, 4096), jnp.floa...  73.9 us

profile of v4, /device:TPU:0, one launch (start us, length us, event | category | flops | bytes accessed | tf_op | source)
XLA Modules:
  0.0 77.3 jit_solution(1371257065382351111)
XLA Ops:
  0.0 0.7 dynamic-slice_bitcast_fusion.1
  0.8 0.3 fusion.9
  1.1 0.2 select_reduce_fusion.1
  1.3 0.6 pad_add_fusion.refs_0_
  1.9 73.9 %shard_map.73 = f32[8,4096]{1,0:T(8,128)} custom-call(s32[4,128]{1,0:T(4,128)} %pad_add_fusion.refs_0_, s32[256]{0:T(256)} %refs_1_.1, bf16[16,2048]{1,0:T(8,128)(2,1)} %bitcast.29, bf16[16,2048,128]{2,1,0:T(8,128)(2,1)} %bitcast.26, bf16[16,2048,128]{2,1,0:T(8,128)(2,1)} %bitcast.27, bf16[128,128,128]{2,1,0:T(8,128)(2,1)} %bitcast.28, bf16[128,128]{1,0:T(8,128)(2,1)} %bitcast.30), custom_call_target="tpu_custom_call" | custom-call | tf_op jit(solution)/shard_map/pallas_call | solution.py:427
  75.8 1.5 %convert_element_type.3 = bf16[8,4096]{1,0:T(8,128)(2,1)} convert(f32[8,4096]{1,0:T(8,128)} %shard_map.73) | non-fusion elementwise | flops 32768 | bytes 196608 | tf_op jit(solution)/shard_map/convert_element_type | solution.py:448
  (8 shorter events, 0.1 us)

commit v5 on v4

--- a/solution.py
+++ b/solution.py
@@ -18,24 +18,32 @@
 MESH = pl.DeviceIdType.MESH
 
 
-def tile_table(slot_tiles, grp, tp):
-    core = grp % 2
-    own = lax.dynamic_index_in_dim(slot_tiles, grp * 32 + tp, 0, keepdims=False)
-    other = lax.dynamic_index_in_dim(
-        slot_tiles, (grp + 1 - 2 * core) * 32 + tp, 0, keepdims=False
+def tile_table(own, other, core):
+    shape = (TILES, TILES)
+    spot = lax.broadcasted_iota(jnp.int32, shape, 0)
+    lane = lax.broadcasted_iota(jnp.int32, shape, 1)
+
+    def as_row(column):
+        return jnp.sum(jnp.where(spot == lane, column, 0), axis=0, keepdims=True)
+
+    x_lo = (spot >> 1) & 1
+    held = jnp.where(
+        (spot & 1) == 0, jnp.broadcast_to(own, shape), jnp.broadcast_to(other, shape)
     )
-    spot = lax.broadcasted_iota(jnp.int32, (TILES, TILES), 0)
-    slot = lax.broadcasted_iota(jnp.int32, (TILES, TILES), 1)
-    owner = ((spot // 2) % 2 * 2 + core) * 32 + spot // 4
-    held = jnp.where(spot % 2 == 0, own[None], other[None])
-    packed = slot * 128 + held % 128
-    packed = jnp.sum(jnp.where(held // 128 == owner, packed, 0), axis=1)
-    index = jnp.arange(TILES, dtype=jnp.int32)
-    key = index // 2 % 2 * 32 + packed % 32
-    before = (key[None] == key[:, None]) & (index[None] < index[:, None])
-    previous = jnp.max(jnp.where(before, index[None], -1), axis=1)
-    last = jnp.max(jnp.where(key[None] == index[:, None], index[None], -1), axis=1)
-    return jnp.stack([packed // 128, packed % 128 // 32, previous, last])
+    match = (held >> 7) == (x_lo * 2 + core) * 32 + (spot >> 2)
+    packed = jnp.max(jnp.where(match, lane * 128 + (held & 127), 0), axis=1, keepdims=True)
+    packed = jnp.broadcast_to(packed, shape)
+    key = x_lo * 32 + (packed & 31)
+    key_row = jnp.broadcast_to(as_row(key), shape)
+    before = (key_row == key) & (lane < spot)
+    previous = jnp.max(jnp.where(before, lane, -1), axis=1, keepdims=True)
+    last = jnp.max(jnp.where(key_row == spot, lane, -1), axis=1, keepdims=True)
+    return [
+        as_row(packed >> 7),
+        as_row((packed >> 5) & 3),
+        as_row(jnp.broadcast_to(previous, shape)),
+        as_row(jnp.broadcast_to(last, shape)),
+    ]
 
 
 def order_of(p, core):
@@ -43,13 +51,14 @@
 
 
 def kernel(*refs):
-    table, lengths, queries, keys, values, tiles_own, scales_own, out = refs[:8]
+    slot_tiles, lengths, queries, keys, values, tiles_own, scales_own, out = refs[:8]
     scratch = list(refs[8:])
     feats = [scratch.pop(0) for _ in range(3)]
     sends = [scratch.pop(0) for _ in range(3)]
     lands = [[[scratch.pop(0) for _ in range(many)] for many in (4, 1, 1)] for _ in range(3)]
     tiles, scales, weights, sums = [scratch.pop(0) for _ in range(4)]
     key_buf, value_buf, att, scales_other, by_row = [scratch.pop(0) for _ in range(5)]
+    table_vmem, table, table_sem = [scratch.pop(0) for _ in range(3)]
     kv_sem, swap_send, swap_recv = [scratch.pop(0) for _ in range(3)]
     load_sem, ag_send, ag_recv, sib_send, sib_recv, rs_send, rs_recv = scratch
 
@@ -114,6 +123,13 @@
         copy.start()
         pending.append(copy)
         return copy
+
+    own = slot_tiles[pl.ds(grp * 32 + tp, 1), :]
+    other = slot_tiles[pl.ds((grp + 1 - 2 * core) * 32 + tp, 1), :]
+    for number, row in enumerate(tile_table(own, other, core)):
+        table_vmem[number : number + 1, :] = row
+    table_load = pltpu.make_async_copy(table_vmem, table, table_sem.at[0])
+    table_load.start()
 
     for h in range(HEADS):
         head = queries[:, h * HEAD_DIM : (h + 1) * HEAD_DIM].astype(jnp.float32)
@@ -217,6 +233,7 @@
         pass_on(p, 2, gather_view(p, moved(p, 2, 1), 1))
     for load in loads:
         load.wait()
+    table_load.wait()
     for swap in swaps:
         swap.wait_recv()
     scales[0] = scales_own[...].astype(jnp.float32)
@@ -248,8 +265,6 @@
         for number in range(7):
             size = feats[p].at[core, 0] if number == 0 else feats[p].at[core, 0, pl.ds(0, 2)]
             remote(size, size, sib_send.at[p, number], sib_recv.at[p, number], sibling).wait_recv()
-
-    for p in range(3):
 
         def multiply(step, carry, p=p):
             for k in range(8):
@@ -319,11 +334,14 @@
         offset = 2 if half == 1 else 0
 
         def step(k, carry):
+            totals = []
             for m in range(4):
                 total = sends[p][at, offset + k, m].astype(jnp.float32)
                 for piece in pieces:
                     total = total + piece[k, m].astype(jnp.float32)
-                sends[p][at, offset + k, m] = total.astype(jnp.bfloat16)
+                totals.append(total.astype(jnp.bfloat16))
+            for m in range(4):
+                sends[p][at, offset + k, m] = totals[m]
             return carry
 
         lax.fori_loop(0, 4 if half is None else 2, step, 0)
@@ -366,11 +384,14 @@
         for copy in direct[p]:
             copy.wait_recv()
         base = tuple(spots[p][:2])
+        totals = []
         for k in range(4):
             total = sends[p][base + (k,)].astype(jnp.float32)
             for by in range(3):
                 total = total + lands[p][1][0][by, k].astype(jnp.float32)
-            sends[p][base + (k,)] = total.astype(jnp.bfloat16)
+            totals.append(total.astype(jnp.bfloat16))
+        for k in range(4):
+            sends[p][base + (k,)] = totals[k]
         last.append(scatter_direct(p, 2))
     for p in range(3):
         for copy in last[p]:
@@ -381,8 +402,8 @@
             for by in range(3):
                 total = total + lands[p][2][0][by, unit].astype(jnp.float32)
             column = (STARTS[p] + unit) * 2 * LANES
-            out[:, column : column + LANES] = total[:8]
-            out[:, column + LANES : column + 2 * LANES] = total[8:]
+            out[:, column : column + LANES] = total[:8].astype(jnp.bfloat16)
+            out[:, column + LANES : column + 2 * LANES] = total[8:].astype(jnp.bfloat16)
 
     for copy in pending:
         copy.wait_send()
@@ -406,6 +427,9 @@
         pltpu.VMEM((HEADS, 16, LANES), jnp.float32),
         pltpu.VMEM((TILES, LANES), bf16),
         pltpu.VMEM((16, HEADS, LANES), jnp.float32),
+        pltpu.VMEM((8, TILES), jnp.int32),
+        pltpu.SMEM((8, TILES), jnp.int32),
+        pltpu.SemaphoreType.DMA((1,)),
         pltpu.SemaphoreType.DMA((2, 2)),
         pltpu.SemaphoreType.DMA((2,)),
         pltpu.SemaphoreType.DMA((2,)),
@@ -421,14 +445,12 @@
 
 
 def body(queries, cache_keys, cache_values, lengths, old_tiles, old_scales, slot_tiles):
-    grp, tp = lax.axis_index("grp"), lax.axis_index("tp")
-    table = tile_table(slot_tiles, grp, tp)
     vmem = pl.BlockSpec(memory_space=pltpu.VMEM)
-    result = pl.pallas_call(
+    return pl.pallas_call(
         kernel,
-        out_shape=jax.ShapeDtypeStruct((8, 4096), jnp.float32),
+        out_shape=jax.ShapeDtypeStruct((8, 4096), jnp.bfloat16),
         in_specs=[
-            pl.BlockSpec(memory_space=pltpu.SMEM),
+            vmem,
             pl.BlockSpec(memory_space=pltpu.SMEM),
             vmem,
             pl.BlockSpec(memory_space=pl.ANY),
@@ -442,10 +464,9 @@
             collective_id=0, has_side_effects=True, vmem_limit_bytes=58 * 2**20
         ),
     )(
-        table, lengths, queries[0], cache_keys[0], cache_values[0],
+        slot_tiles, lengths, queries[0], cache_keys[0], cache_values[0],
         old_tiles[0], old_scales[0],
     )
-    return result.astype(jnp.bfloat16)
 
 
 def solution(mesh):

time: 78 us -> 76.1 us (0.976)
  other arithmetic: 2.68 us -> 0 us
    convert_element_type x1 -> x0, other arithmetic: 1.54 us -> none  [body(): return result.astype(jnp.bfloat16)]
    unnamed x0 -> x1, local copies, waits for them, and re-layouts: none -> 1.47 us
where the time goes in v5:
time: 76.1 us; the launch traced here: 75 us
  Pallas kernels  73.6 us (97%)
  local copies, waits for them, and re-layouts  1.47 us (2%)
    pallas_call x1, Pallas kernels, body(): pl.pallas_call(kernel, out_shape=jax.ShapeDtypeStruct((8, 4096), jnp.bflo...  73.6 us

profile of v5, /device:TPU:0, one launch (start us, length us, event | category | flops | bytes accessed | tf_op | source)
XLA Modules:
  0.0 75.0 jit_solution(1398895157935276800)
XLA Ops:
  0.0 73.6 %shard_map.73 = bf16[8,4096]{1,0:T(8,128)(2,1)} custom-call(s32[128,128]{1,0:T(8,128)} %refs_0_.1, s32[256]{0:T(256)} %refs_1_.1, bf16[16,2048]{1,0:T(8,128)(2,1)} %bitcast.8, bf16[16,2048,128]{2,1,0:T(8,128)(2,1)} %bitcast.5, bf16[16,2048,128]{2,1,0:T(8,128)(2,1)} %bitcast.6, bf16[128,128,128]{2,1,0:T(8,128)(2,1)} %bitcast.7, bf16[128,128]{1,0:T(8,128)(2,1)} %bitcast.9), custom_call_target="tpu_custom_call" | custom-call | tf_op jit(solution)/shard_map/pallas_call | solution.py:449
  73.6 1.5 %copy.9 = bf16[8,4096]{1,0:T(8,128)(2,1)} copy(bf16[8,4096]{1,0:T(8,128)(2,1)} %shard_map.73) | data formatting | bytes 131072

commit v6 on v5

--- a/solution.py
+++ b/solution.py
@@ -272,13 +272,18 @@
                 part = table[1, spot]
                 columns = []
                 for j in range(2):
+                    found = []
+                    for c in range(2):
+                        at = {"x": pl.ds(part // 2 * 2, 2), "y": pl.ds(0, 4), "z": part % 2 * 2 + j}
+                        first, second, third = order_of(p, c)
+                        found.append(feats[p][c, at[third], at[second], at[first], step])
                     blocks = []
                     for x_lo in range(2):
                         for c in range(2):
+                            order = order_of(p, c)
+                            x_outer = order.index("x") > order.index("y")
                             for y in range(4):
-                                at = {"x": part // 2 * 2 + x_lo, "y": y, "z": part % 2 * 2 + j}
-                                first, second, third = order_of(p, c)
-                                blocks.append(feats[p][c, at[third], at[second], at[first], step])
+                                blocks.append(found[c][x_lo, y] if x_outer else found[c][y, x_lo])
                     columns.append(jnp.concatenate(blocks, axis=0))
                 left = jnp.concatenate(columns, axis=1)
                 weight = weights[spot]
@@ -349,21 +354,25 @@
     copies = []
     for p in range(3):
 
-        def lay_out(step, carry, p=p):
-            for x_lo in range(2):
-                pair = []
-                for k in range(2):
-                    link = table[3, x_lo * 32 + (STARTS[p] + step) * 2 + k]
-                    pair.append(jnp.where(link >= 0, sums[jnp.maximum(link, 0)], 0.0))
-                for t in range(32):
-                    at = {"x": t // 4 % 2 * 2 + x_lo, "y": t // 8, "z": t % 4}
-                    zero, one = order_of(p, 0), order_of(p, 1)
-                    first, second, third = (either(at[a], at[b]) for a, b in zip(zero, one))
-                    unit = jnp.concatenate([half[8 * t : 8 * t + 8] for half in pair], axis=0)
-                    sends[p][first, second, third, step] = unit.astype(jnp.bfloat16)
-            return carry
-
-        lax.fori_loop(0, COUNTS[p], lay_out, 0)
+        for c in range(2):
+
+            def lay_out(step, carry, p=p, c=c):
+                for x_lo in range(2):
+                    pair = []
+                    for k in range(2):
+                        link = table[3, x_lo * 32 + (STARTS[p] + step) * 2 + k]
+                        pair.append(jnp.where(link >= 0, sums[jnp.maximum(link, 0)], 0.0))
+                    for t in range(32):
+                        at = {"x": t // 4 % 2 * 2 + x_lo, "y": t // 8, "z": t % 4}
+                        first, second, third = order_of(p, c)
+                        unit = jnp.concatenate([half[8 * t : 8 * t + 8] for half in pair], axis=0)
+                        sends[p][at[first], at[second], at[third], step] = unit.astype(jnp.bfloat16)
+                return carry
+
+            @pl.when(core == c)
+            def _(p=p, lay_out=lay_out):
+                lax.fori_loop(0, COUNTS[p], lay_out, 0)
+
         copies.append(scatter_start(p))
 
     for p in range(3):

time: 76.1 us -> 74.8 us (0.983)
  no operation moved by 1% of the time
where the time goes in v6:
time: 74.8 us; the launch traced here: 74.5 us
  Pallas kernels  73 us (98%)
  local copies, waits for them, and re-layouts  1.47 us (2%)
    pallas_call x1, Pallas kernels, body(): pl.pallas_call(kernel, out_shape=jax.ShapeDtypeStruct((8, 4096), jnp.bflo...  73 us

profile of v6, /device:TPU:0, one launch (start us, length us, event | category | flops | bytes accessed | tf_op | source)
XLA Modules:
  0.0 74.5 jit_solution(16614553644078161644)
XLA Ops:
  0.0 73.0 %shard_map.73 = bf16[8,4096]{1,0:T(8,128)(2,1)} custom-call(s32[128,128]{1,0:T(8,128)} %refs_0_.1, s32[256]{0:T(256)} %refs_1_.1, bf16[16,2048]{1,0:T(8,128)(2,1)} %bitcast.8, bf16[16,2048,128]{2,1,0:T(8,128)(2,1)} %bitcast.5, bf16[16,2048,128]{2,1,0:T(8,128)(2,1)} %bitcast.6, bf16[128,128,128]{2,1,0:T(8,128)(2,1)} %bitcast.7, bf16[128,128]{1,0:T(8,128)(2,1)} %bitcast.9), custom_call_target="tpu_custom_call" | custom-call | tf_op jit(solution)/shard_map/pallas_call | solution.py:458
  73.0 1.5 %copy.9 = bf16[8,4096]{1,0:T(8,128)(2,1)} copy(bf16[8,4096]{1,0:T(8,128)(2,1)} %shard_map.73) | data formatting | bytes 131072

commit v7 on v6

--- a/solution.py
+++ b/solution.py
@@ -255,8 +255,8 @@
         return carry
 
     lax.fori_loop(0, TILES // 8, dequantize, 0)
-    for p in range(3):
-        for number in (2, 3, 4, 5):
+    for numbers, p in [((2, 3), p) for p in range(3)] + [((4, 5), p) for p in range(3)]:
+        for number in numbers:
             founds[p][number].wait_recv()
             by, half = ((3, 1), (1, 0), (2, 0), (2, 1))[number - 2]
             pass_on(p, number + 1, gather_view(p, moved(p, 2, by), half))
@@ -267,6 +267,7 @@
             remote(size, size, sib_send.at[p, number], sib_recv.at[p, number], sibling).wait_recv()
 
         def multiply(step, carry, p=p):
+            terms = []
             for k in range(8):
                 spot = (STARTS[p] + step) * 8 + k
                 part = table[1, spot]
@@ -292,10 +293,13 @@
                     weight = jnp.concatenate([weight[:64], none, weight[64:], none], axis=0)
                 else:
                     weight = jnp.concatenate([none, weight[:64], none, weight[64:]], axis=0)
-                term = jnp.dot(left, weight, preferred_element_type=jnp.float32)
-                link = table[2, spot]
-                earlier = sums[jnp.maximum(link, 0)]
-                sums[spot] = term + jnp.where(link >= 0, earlier, 0.0)
+                terms.append((spot, jnp.dot(left, weight, preferred_element_type=jnp.float32)))
+                if k % 8 == 7:
+                    for spot, term in terms:
+                        link = table[2, spot]
+                        earlier = sums[jnp.maximum(link, 0)]
+                        sums[spot] = term + jnp.where(link >= 0, earlier, 0.0)
+                    terms = []
             return carry
 
         lax.fori_loop(0, COUNTS[p], multiply, 0)

time: 74.8 us -> 74.7 us (level)
  no operation moved by 1% of the time
where the time goes in v7:
time: 74.7 us; the launch traced here: 74.4 us
  Pallas kernels  72.9 us (98%)
  local copies, waits for them, and re-layouts  1.47 us (2%)
    pallas_call x1, Pallas kernels, body(): pl.pallas_call(kernel, out_shape=jax.ShapeDtypeStruct((8, 4096), jnp.bflo...  72.9 us

profile of v7, /device:TPU:0, one launch (start us, length us, event | category | flops | bytes accessed | tf_op | source)
XLA Modules:
  0.0 74.4 jit_solution(6011784032378233483)
XLA Ops:
  0.0 72.9 %shard_map.73 = bf16[8,4096]{1,0:T(8,128)(2,1)} custom-call(s32[128,128]{1,0:T(8,128)} %refs_0_.1, s32[256]{0:T(256)} %refs_1_.1, bf16[16,2048]{1,0:T(8,128)(2,1)} %bitcast.8, bf16[16,2048,128]{2,1,0:T(8,128)(2,1)} %bitcast.5, bf16[16,2048,128]{2,1,0:T(8,128)(2,1)} %bitcast.6, bf16[128,128,128]{2,1,0:T(8,128)(2,1)} %bitcast.7, bf16[128,128]{1,0:T(8,128)(2,1)} %bitcast.9), custom_call_target="tpu_custom_call" | custom-call | tf_op jit(solution)/shard_map/pallas_call | solution.py:462
  72.9 1.5 %copy.9 = bf16[8,4096]{1,0:T(8,128)(2,1)} copy(bf16[8,4096]{1,0:T(8,128)(2,1)} %shard_map.73) | data formatting | bytes 131072

commit v8 on v7

--- a/solution.py
+++ b/solution.py
@@ -255,8 +255,8 @@
         return carry
 
     lax.fori_loop(0, TILES // 8, dequantize, 0)
-    for numbers, p in [((2, 3), p) for p in range(3)] + [((4, 5), p) for p in range(3)]:
-        for number in numbers:
+    for p in range(3):
+        for number in (2, 3, 4, 5):
             founds[p][number].wait_recv()
             by, half = ((3, 1), (1, 0), (2, 0), (2, 1))[number - 2]
             pass_on(p, number + 1, gather_view(p, moved(p, 2, by), half))

time: 74.7 us -> 74.8 us (level)
  no operation moved by 1% of the time
where the time goes in v8:
time: 74.8 us; the launch traced here: 74.5 us
  Pallas kernels  73 us (98%)
  local copies, waits for them, and re-layouts  1.47 us (2%)
    pallas_call x1, Pallas kernels, body(): pl.pallas_call(kernel, out_shape=jax.ShapeDtypeStruct((8, 4096), jnp.bflo...  73 us

profile of v8, /device:TPU:0, one launch (start us, length us, event | category | flops | bytes accessed | tf_op | source)
XLA Modules:
  0.0 74.5 jit_solution(16614553644078161644)
XLA Ops:
  0.0 73.0 %shard_map.73 = bf16[8,4096]{1,0:T(8,128)(2,1)} custom-call(s32[128,128]{1,0:T(8,128)} %refs_0_.1, s32[256]{0:T(256)} %refs_1_.1, bf16[16,2048]{1,0:T(8,128)(2,1)} %bitcast.8, bf16[16,2048,128]{2,1,0:T(8,128)(2,1)} %bitcast.5, bf16[16,2048,128]{2,1,0:T(8,128)(2,1)} %bitcast.6, bf16[128,128,128]{2,1,0:T(8,128)(2,1)} %bitcast.7, bf16[128,128]{1,0:T(8,128)(2,1)} %bitcast.9), custom_call_target="tpu_custom_call" | custom-call | tf_op jit(solution)/shard_map/pallas_call | solution.py:462
  73.0 1.5 %copy.9 = bf16[8,4096]{1,0:T(8,128)(2,1)} copy(bf16[8,4096]{1,0:T(8,128)(2,1)} %shard_map.73) | data formatting | bytes 131072
